TPU v7x, 128 devices: a whole 4x4x4 slice. The times are simulated.
128 devices in a mesh: tm: 16 (over z, y), space: 8 (over x, core).
Axes of the slice: x: 4, y: 4, z: 4, core: 2. Of those that a mesh axis runs over, the one named last changes fastest.
Arguments:
- start_state: float32 [4, 32768], P(None, 'space'), may hold values from -6 to 6
- guess: float32 [16, 4, 32768], P('tm', None, 'space'), may hold values from -6 to 6
- diag_blocks: bfloat16 [256, 128, 128], P('space'), may hold values from -3 to 1
- off_blocks: bfloat16 [256, 4, 128, 128], P('space'), may hold values from -0.125 to 0.125
- columns: int32 [256, 4], P('space'), may hold values from 0 to 255, as said below
- rates: float32 [32768], P('space'), may hold values from 0.2 to 2
- mixing: float32 [4, 4], replicated, may hold values from -3 to 3
- fine_inverse: bfloat16 [256, 128, 128], P('space'), may hold values from -1 to 2
- coarse_inverse: bfloat16 [256, 128, 128], P('space'), may hold values from -1 to 2
Outputs:
- node_values: float32 [16, 3, 4, 32768], P('tm', None, None, 'space')
Inputs may be any that keep to these rules, and one draw needn't show every extreme that they name: `columns`: each entry lies within 8 blocks of its row's block; both -8 and +8 are reached by some row.
All inputs are finite; a program needn't handle non-finite values.
Results may differ from a plain program's by a relative error of at most 0.02.
Values may be sent and summed in bfloat16 or wider, within the bound.
A program may use at most 64 MiB of HBM per device.

v0:
```python
import jax
import jax.numpy as jnp
from jax import lax
from jax.sharding import PartitionSpec as P

BS = 128
SPECIES = 4
ITERS = 2
W = 8


STEP = 0.25


def extended(cells, sides, width):
    for axis, dim in sides:
        count = lax.axis_size(axis)
        ends = count - 1
        head = lax.slice_in_dim(cells, 0, width, axis=dim)
        tail = lax.slice_in_dim(cells, cells.shape[dim] - width, cells.shape[dim], axis=dim)
        cells = jnp.concatenate(
            [
                lax.ppermute(tail, axis, [(i, (i + 1) % count) for i in range(ends)]),
                cells,
                lax.ppermute(head, axis, [((i + 1) % count, i) for i in range(ends)]),
            ],
            axis=dim,
        )
    return cells


def from_behind(block, axis, distance):
    devices = range(lax.axis_size(axis))
    route = [(i - distance, i) for i in devices if i - distance in devices]
    return lax.ppermute(block, axis, route)


def products(field, narrow, widened, local_columns, diag_blocks, off_blocks, rates, mixing):
    node_count = field.shape[0]
    block_rows = diag_blocks.shape[0]
    widened_blocks = widened.reshape(node_count, SPECIES, -1, BS)
    nearby = jnp.take(widened_blocks, local_columns, axis=2)
    own_blocks = narrow.reshape(node_count, SPECIES, block_rows, BS)
    implicit = jnp.einsum(
        "bij,nsbj->nsbi", diag_blocks, own_blocks, preferred_element_type=jnp.float32
    )
    explicit = jnp.einsum(
        "bkij,nsbkj->nsbi", off_blocks, nearby, preferred_element_type=jnp.float32
    )
    reaction = jnp.einsum("st,ntc->nsc", mixing, field, precision=lax.Precision.HIGHEST) * rates
    implicit = implicit.reshape(field.shape)
    explicit = explicit.reshape(field.shape) + reaction
    return (implicit, explicit)


def evaluate(field, diag_blocks, off_blocks, columns, rates, mixing):
    block_rows = diag_blocks.shape[0]
    narrow = field.astype(jnp.bfloat16)
    widened = extended(narrow, (("space", 2),), W * BS)
    local_columns = columns - (lax.axis_index("space") * block_rows - W)
    return products(field, narrow, widened, local_columns, diag_blocks, off_blocks, rates, mixing)


def apply_inverse(rhs, inverse_blocks):
    block_rows = inverse_blocks.shape[0]
    narrow = rhs.astype(jnp.bfloat16).reshape(SPECIES, block_rows, BS)
    solved = jnp.einsum("bij,sbj->sbi", inverse_blocks, narrow, preferred_element_type=jnp.float32)
    return solved.reshape(rhs.shape)


def shards(
    start_state,
    guess,
    diag_blocks,
    off_blocks,
    columns,
    rates,
    mixing,
    fine_inverse,
    coarse_inverse,
):
    first_slice = lax.axis_index("tm") == 0
    section_count = lax.axis_size("tm")
    half_step = STEP / 2

    def terms(field):
        return evaluate(field, diag_blocks, off_blocks, columns, rates, mixing)

    def single_terms(field):
        implicit, explicit = terms(field[None])
        return (implicit[0], explicit[0])

    initial = guess[0]
    node_values = jnp.stack([jnp.where(first_slice, start_state, initial), initial, initial])
    implicit_now, explicit_now = terms(node_values)
    for sweep_round in range(ITERS):
        forces = implicit_now + explicit_now
        rhs_one = (
            node_values[0]
            - half_step * implicit_now[1]
            + STEP * (5.0 / 24.0 * forces[0] + 1.0 / 3.0 * forces[1] - 1.0 / 24.0 * forces[2])
        )
        node_one = apply_inverse(rhs_one, fine_inverse)
        imp_one, exp_one = single_terms(node_one)
        rhs_two = (
            node_one
            + half_step * (exp_one - explicit_now[1])
            - half_step * implicit_now[2]
            + STEP * (-1.0 / 24.0 * forces[0] + 1.0 / 3.0 * forces[1] + 5.0 / 24.0 * forces[2])
        )
        node_two = apply_inverse(rhs_two, fine_inverse)
        imp_two, exp_two = single_terms(node_two)
        one_force = imp_one + exp_one
        two_force = imp_two + exp_two
        fas_term = STEP * (2.0 / 3.0 * one_force - 1.0 / 3.0 * forces[0] - 1.0 / 3.0 * two_force)
        head_force = forces[0]
        head_explicit = explicit_now[0]

        def coarse_sweeps(start_value, start_imp, start_exp):
            rhs_first = (
                start_value
                + STEP * (start_exp - head_explicit)
                - STEP * imp_two
                + STEP / 2 * (head_force + two_force)
                + fas_term
            )
            middle = apply_inverse(rhs_first, coarse_inverse)
            mid_imp, mid_exp = single_terms(middle)
            rhs_second = (
                start_value
                - STEP * mid_imp
                + STEP / 2 * (start_imp + start_exp + (mid_imp + mid_exp))
                + fas_term
            )
            return apply_inverse(rhs_second, coarse_inverse)

        blank = jnp.zeros_like(start_state)

        def advance(section_index, carry):
            received = from_behind(carry[0], "tm", 1)
            start_value = jnp.where(first_slice, start_state, received)
            start_imp, start_exp = single_terms(start_value)
            end_value = coarse_sweeps(start_value, start_imp, start_exp)
            return (end_value, start_value)

        final_value, start_value = lax.fori_loop(0, section_count, advance, (blank, blank))
        middle_new = node_one + 0.5 * (start_value - node_values[0] + (final_value - node_two))
        node_values = jnp.stack([start_value, middle_new, final_value])
        implicit_now, explicit_now = terms(node_values)
    return node_values[None]


def solution(mesh):
    in_specs = (
        P(None, "space"),
        P("tm", None, "space"),
        P("space", None, None),
        P("space", None, None, None),
        P("space", None),
        P("space"),
        P(),
        P("space", None, None),
        P("space", None, None),
    )
    out_specs = P("tm", None, None, "space")
    return jax.shard_map(shards, mesh=mesh, in_specs=in_specs, out_specs=out_specs, check_vma=False)
```

profile of v0, /device:TPU:120, one launch (start us, length us, event | category | flops | bytes accessed | tf_op | source)
XLA Modules:
  0.0 1207.2 jit_solution(9297167862809670695)
XLA Ops:
  44.5 548.3 %while.28 = (s32[]{:T(128)}, f32[4,4096]{1,0:T(4,128)}, f32[4,4096]{1,0:T(4,128)}, pred[]{:T(512)}, f32[4,4096]{1,0:T(4,128)S(1)}, /*index=5*/s32[32,4]{0,1:T(4,...) while((s32[]{:T(128)}, f32[4,4096]{1,0:T(4,128)}, ...), condition=%wide.region_1.4_spmd, body=%wide.region_0.0_spmd.sunk | while | flops 52758404 | bytes 16754426 | solution.py:146
  46.1 4.9 collective-permute-done
  78.4 4.9 collective-permute-done
  210.1 6.9 collective-permute-done
  245.0 7.0 collective-permute-done
  280.1 6.9 collective-permute-done
  315.0 6.8 collective-permute-done
  349.9 6.7 collective-permute-done
  384.7 6.7 collective-permute-done
  419.4 6.7 collective-permute-done
  454.2 7.0 collective-permute-done
  489.2 7.0 collective-permute-done
  524.3 7.0 collective-permute-done
  559.4 7.0 collective-permute-done
  612.2 5.0 collective-permute-start.18
  643.5 561.1 %while.29 = (s32[]{:T(128)}, f32[4,4096]{1,0:T(4,128)}, f32[4,4096]{1,0:T(4,128)}, pred[]{:T(512)}, f32[4,4096]{1,0:T(4,128)S(1)}, /*index=5*/s32[32,4]{0,1:T(4,...) while((s32[]{:T(128)}, f32[4,4096]{1,0:T(4,128)}, ...), condition=%wide.region_3.6_spmd, body=%wide.region_2.5_spmd.sunk | while | flops 52758404 | bytes 17016596 | solution.py:146
  645.0 7.0 collective-permute-done.5
  679.9 7.0 collective-permute-done.5
  715.1 7.0 collective-permute-done.5
  750.2 6.7 collective-permute-done.5
  785.1 7.0 collective-permute-done.5
  820.3 7.0 collective-permute-done.5
  855.5 7.0 collective-permute-done.5
  890.7 7.0 collective-permute-done.5
  925.8 7.0 collective-permute-done.5
  961.0 6.9 collective-permute-done.5
  996.1 6.8 collective-permute-done.5
  1031.1 6.7 collective-permute-done.5
  1065.9 6.7 collective-permute-done.5
  1100.8 6.7 collective-permute-done.5
  1135.7 7.0 collective-permute-done.5
  1170.9 7.0 collective-permute-done.5
  (1296 shorter events, 1000.3 us)
Async XLA Ops:
  96.0 8.5 collective-permute-start.3
  129.0 8.4 collective-permute-start.3
  162.0 8.4 collective-permute-start.3
  195.0 8.2 collective-permute-start.3
  208.6 8.4 collective-permute-start
  243.5 8.5 collective-permute-start
  278.6 8.4 collective-permute-start
  313.5 8.3 collective-permute-start
  348.4 8.2 collective-permute-start
  383.2 8.2 collective-permute-start
  417.9 8.2 collective-permute-start
  452.7 8.5 collective-permute-start
  487.7 8.5 collective-permute-start
  522.8 8.5 collective-permute-start
  544.3 8.1 collective-permute-start.3
  557.8 8.5 collective-permute-start
  643.5 8.5 collective-permute-start.5
  678.4 8.5 collective-permute-start.5
  713.6 8.5 collective-permute-start.5
  748.7 8.2 collective-permute-start.5
  783.6 8.5 collective-permute-start.5
  818.8 8.5 collective-permute-start.5
  854.0 8.5 collective-permute-start.5
  889.2 8.5 collective-permute-start.5
  924.3 8.5 collective-permute-start.5
  959.5 8.4 collective-permute-start.5
  994.6 8.3 collective-permute-start.5
  1029.6 8.2 collective-permute-start.5
  1064.4 8.2 collective-permute-start.5
  1099.3 8.2 collective-permute-start.5
  1134.2 8.5 collective-permute-start.5
  1169.4 8.5 collective-permute-start.5
  (278 other events, 2170.0 us)
where the time goes:
time: 1230 us; the launch traced here: 1210 us
  matrix products  463 us (38%)
  starting transfers between devices  416 us (34%)
  waiting for transfers between devices  228 us (19%)
  local copies, waits for them, and re-layouts  79.5 us (6%)
  other arithmetic  13.8 us (1%)
    ppermute x70, starting transfers between devices, extended(): lax.ppermute(tail, axis, [(i, (i + 1) % count) for i in range(ends)])  285 us
    ppermute x32, waiting for transfers between devices, from_behind(): return lax.ppermute(block, axis, route)  210 us
    dot_general x68, matrix products, apply_inverse(): jnp.einsum('bij,sbj->sbi', inverse_blocks, narrow, preferred_element_type...  199 us
    dot_general x38, matrix products, products(): jnp.einsum('bkij,nsbkj->nsbi', off_blocks, nearby, preferred_element_type...  132 us
    dot_general x70, matrix products, products(): jnp.einsum('bij,nsbj->nsbi', diag_blocks, own_blocks, preferred_element_t...  91.7 us
    ppermute x70, starting transfers between devices, extended(): lax.ppermute(head, axis, [((i + 1) % count, i) for i in range(ends)])  90.6 us
    gather x72, local copies, waits for them, and re-layouts, products(): nearby = jnp.take(widened_blocks, local_columns, axis=2)  55.4 us
    ppermute x32, starting transfers between devices, from_behind(): return lax.ppermute(block, axis, route)  41 us
  transfers between devices with their start and end apart: 172, of which 69 were waited for; matrix products, arithmetic and copies ran while one was open for 9% of the time, Pallas kernels for 0%

commit v1 on v0

v1 whole, which is shorter than its diff:
```python
import functools

import jax
import jax.numpy as jnp
from jax import lax
from jax.experimental import pallas as pl
from jax.experimental.pallas import tpu as pltpu
from jax.sharding import PartitionSpec as P

BS = 128
K = 4
SPECIES = 4
ITERS = 2
W = 8
STEP = 0.25
HALF = STEP / 2
MESH = pl.DeviceIdType.MESH
NODES, FIRST, SECOND, MIDDLE = range(4)
LEFT, RIGHT = 0, 1


def dot(lhs, rhs):
    return lax.dot_general(
        lhs.astype(jnp.bfloat16), rhs, (((1,), (0,)), ((), ())), preferred_element_type=jnp.float32
    )


def rows_loop(first, last, body):
    def step(i, carry):
        body(i)
        return carry

    lax.fori_loop(first, last, step, 0, unroll=True)


def kernel(
    n_tm, n_sp, rows,
    start, guess, cols, rates, mixing, diag_h, off_h, fine_h, coarse_h,
    out,
    diag_v, off_v, fine_v, coarse_v, raw_w, fine_w, comp_w,
    near, near_q, mix_v, nodes, imp_b, exp_b, mid_b, first_v, second_r,
    sum_c, sum_t, state, grown, partial, fresh,
    send_b, land, own_send, s_land, s_halo,
    place_of, load_sem, send_sem, recv_sem, s_send_sem, s_recv_sem,
):
    tm = lax.axis_index("tm")
    sp = lax.axis_index("space")
    base = sp * rows - W
    has_left, has_right = sp > 0, sp < n_sp - 1
    edge = W // 4

    loads = [
        pltpu.make_async_copy(src, dst, load_sem.at[i])
        for i, (src, dst) in enumerate(
            ((diag_h, diag_v), (off_h, off_v), (fine_h, fine_v), (coarse_h, coarse_v))
        )
    ]
    for load in loads:
        load.start()

    barrier = pltpu.get_barrier_semaphore()

    def greet(t, s, there):
        @pl.when(there)
        def _():
            pl.semaphore_signal(barrier, inc=1, device_id=(t, s), device_id_type=MESH)

    up, down = tm < n_tm - 1, tm > 0
    others = [
        (tm, sp - 1, has_left), (tm, sp + 1, has_right),
        (tm + 1, sp, up), (tm - 1, sp, down),
        (tm + 1, sp - 1, up & has_left), (tm + 1, sp + 1, up & has_right),
        (tm - 1, sp - 1, down & has_left), (tm - 1, sp + 1, down & has_right),
    ]
    for other in others:
        greet(*other)

    def local_place(b, carry):
        for k in range(K):
            place_of[b, k] = jnp.clip(cols[b, k] - base, 0, rows + 2 * W - 1)
        return carry

    lax.fori_loop(0, rows, local_place, 0)
    near[...] = jnp.zeros_like(near)
    near_q[...] = jnp.zeros_like(near_q)
    imp_b[...] = jnp.zeros_like(imp_b)
    exp_b[...] = jnp.zeros_like(exp_b)
    mid_b[...] = jnp.zeros_like(mid_b)
    for t in range(SPECIES):
        column = jnp.broadcast_to(mixing[:, t : t + 1], (SPECIES, BS))
        mix_v[t] = jnp.concatenate([column, column], axis=0)

    pl.semaphore_wait(barrier, sum(there.astype(jnp.int32) for _, _, there in others))

    def halo_copies(kind, count):
        to_left = pltpu.make_async_remote_copy(
            src_ref=send_b.at[kind, LEFT, pl.ds(0, count)],
            dst_ref=land.at[kind, RIGHT, pl.ds(0, count)],
            send_sem=send_sem.at[kind, LEFT], recv_sem=recv_sem.at[kind, RIGHT],
            device_id=(tm, sp - 1), device_id_type=MESH,
        )
        to_right = pltpu.make_async_remote_copy(
            src_ref=send_b.at[kind, RIGHT, pl.ds(0, count)],
            dst_ref=land.at[kind, LEFT, pl.ds(0, count)],
            send_sem=send_sem.at[kind, RIGHT], recv_sem=recv_sem.at[kind, LEFT],
            device_id=(tm, sp + 1), device_id_type=MESH,
        )
        return to_left, to_right

    def halo_send(kind, fields):
        for f, field in enumerate(fields):
            for j in range(edge):
                low = [field(4 * j + g) for g in range(4)]
                high = [field(rows - W + 4 * j + g) for g in range(4)]
                send_b[kind, LEFT, f * edge + j] = jnp.concatenate(low, axis=0).astype(jnp.bfloat16)
                send_b[kind, RIGHT, f * edge + j] = jnp.concatenate(high, axis=0).astype(jnp.bfloat16)
        to_left, to_right = halo_copies(kind, edge * len(fields))
        pl.when(has_left)(to_left.start)
        pl.when(has_right)(to_right.start)

    def halo_wait(kind, count):
        to_left, to_right = halo_copies(kind, edge * count)

        @pl.when(has_left)
        def _():
            to_right.wait_recv()
            to_left.wait_send()

        @pl.when(has_right)
        def _():
            to_left.wait_recv()
            to_right.wait_send()

    def spread(tile, target, block, row):
        wide = tile.astype(jnp.float32)
        for g in range(4):
            target[block + g, row : row + 4] = wide[4 * g : 4 * g + 4]

    def halo_place(kind, target, count):
        for f in range(count):
            for j in range(edge):
                spread(land[kind, LEFT, f * edge + j], target, 4 * j, 4 * f)
                spread(land[kind, RIGHT, f * edge + j], target, W + rows + 4 * j, 4 * f)

    def gather(source, b):
        return jnp.concatenate([source[place_of[b, k]] for k in range(K)], axis=1)

    def react(v, b):
        total = None
        for t in range(SPECIES):
            line = v[t : t + 1]
            if v.shape[0] == 8:
                second = v[4 + t : 5 + t]
                row = lax.broadcasted_iota(jnp.int32, (8, BS), 0)
                line = jnp.where(row < 4, jnp.broadcast_to(line, (8, BS)), jnp.broadcast_to(second, (8, BS)))
            term = mix_v[t, : v.shape[0]] * line
            total = term if total is None else total + term
        return total * rates[pl.ds(b, 1)]

    def implicit(b):
        return dot(near[W + b], raw_w[b, :BS])

    def explicit(b, count):
        got = dot(gather(near, b), raw_w[b, BS:])[: 4 * count]
        return got + react(near[W + b, : 4 * count], b)

    def begin(b):
        mine = guess[0, :, pl.ds(pl.multiple_of(b * BS, BS), BS)]
        first = start[:, pl.ds(pl.multiple_of(b * BS, BS), BS)]
        head = jnp.where(tm == 0, first, mine)
        nodes[b, 0:4] = head
        nodes[b, 4:8] = mine

    rows_loop(0, rows, begin)

    def transposed(b, carry):
        raw_w[b, :BS] = diag_v[b].T
        for k in range(K):
            raw_w[b, BS * (k + 1) : BS * (k + 2)] = off_v[b, k].T
        fine_w[b] = fine_v[b].T
        comp_w[b, BS : 2 * BS] = coarse_v[b].T
        return carry

    def composed(b, carry):
        both = dot(raw_w[b], comp_w[b, BS : 2 * BS]) * STEP
        comp_w[b, :BS] = both[:BS].astype(jnp.bfloat16)
        comp_w[b, 2 * BS :] = both[BS:].astype(jnp.bfloat16)
        return carry

    def order(body):
        return lambda: rows_loop(W, rows - W, body), lambda: (
            rows_loop(0, W, body), rows_loop(rows - W, rows, body)
        )

    def s_copies(it):
        return [
            (pltpu.make_async_remote_copy(
                src_ref=own_send.at[it], dst_ref=s_land.at[it],
                send_sem=s_send_sem.at[it, 0], recv_sem=s_recv_sem.at[it, 0],
                device_id=(tm + 1, sp), device_id_type=MESH), up, down),
            (pltpu.make_async_remote_copy(
                src_ref=own_send.at[it, pl.ds(0, edge)], dst_ref=s_halo.at[it, RIGHT],
                send_sem=s_send_sem.at[it, 1], recv_sem=s_recv_sem.at[it, 1],
                device_id=(tm + 1, sp - 1), device_id_type=MESH), up & has_left, down & has_right),
            (pltpu.make_async_remote_copy(
                src_ref=own_send.at[it, pl.ds(rows // 4 - edge, edge)], dst_ref=s_halo.at[it, LEFT],
                send_sem=s_send_sem.at[it, 2], recv_sem=s_recv_sem.at[it, 2],
                device_id=(tm + 1, sp + 1), device_id_type=MESH), up & has_right, down & has_left),
        ]

    def iteration(it, carry):
        halo_send(NODES, [lambda b: nodes[b, 0:4], lambda b: nodes[b, 4:8]])

        @pl.when(it == 0)
        def _():
            for load in loads:
                load.wait()
            lax.fori_loop(0, rows, transposed, 0)

        def place(b):
            near[W + b] = nodes[b]

        rows_loop(0, rows, place)
        own_part = jnp.where(it == 0, 0.0, 0.5)
        end_part = jnp.where(it == 0, 1.0, 0.5)

        def node_terms(b):
            imp = implicit(b)
            exp = explicit(b, 2)
            imp_0, exp_0, imp_2, exp_2 = imp[:4], exp[:4], imp[4:], exp[4:]
            one_i = imp_b[b] + own_part * imp_0 + end_part * imp_2
            one_e = exp_b[b] + own_part * exp_0 + end_part * exp_2
            f_0, f_1, f_2 = imp_0 + exp_0, one_i + one_e, imp_2 + exp_2
            rhs = near[W + b, 0:4] - HALF * one_i + STEP * (5 / 24 * f_0 + 1 / 3 * f_1 - 1 / 24 * f_2)
            second_r[b] = STEP * (-1 / 24 * f_0 + 1 / 3 * f_1 + 5 / 24 * f_2) - HALF * (one_e + imp_2)
            sum_c[b] = STEP * (1 / 6 * f_0 - exp_0)
            sum_t[b] = (-STEP / 3) * f_0
            imp_b[b] = -0.5 * imp_0
            exp_b[b] = -0.5 * exp_0
            first_v[b] = dot(rhs, fine_w[b])

        inner, outer = order(node_terms)
        inner()
        halo_wait(NODES, 2)
        halo_place(NODES, near, 2)
        outer()
        halo_send(FIRST, [lambda b: first_v[b]])

        def put_first(b):
            near[W + b, 0:4] = first_v[b]

        rows_loop(0, rows, put_first)

        def first_terms(b):
            imp = implicit(b)[:4]
            exp = explicit(b, 1)
            force = STEP * 2 / 3 * (imp + exp)
            sum_c[b] += force
            sum_t[b] += force
            imp_b[b] += imp
            exp_b[b] += exp
            fresh[b] = dot(first_v[b] + HALF * exp + second_r[b], fine_w[b])

        inner, outer = order(first_terms)
        inner()
        halo_wait(FIRST, 1)
        halo_place(FIRST, near, 1)
        outer()
        halo_send(SECOND, [lambda b: fresh[b]])

        @pl.when(it == 0)
        def _():
            lax.fori_loop(0, rows, composed, 0)

        def put_second(b):
            near[W + b, 0:4] = fresh[b]
            mid_b[b] = first_v[b] - 0.5 * (nodes[b, 0:4] + fresh[b])

        rows_loop(0, rows, put_second)

        def second_terms(b):
            imp = implicit(b)[:4]
            exp = explicit(b, 1)
            force = imp + exp
            sum_c[b] += STEP * (1 / 6 * force - imp)
            sum_t[b] += (-STEP / 3) * force
            imp_b[b] += -0.5 * imp
            exp_b[b] += -0.5 * exp

        inner, outer = order(second_terms)
        inner()
        halo_wait(SECOND, 1)
        halo_place(SECOND, near, 1)
        outer()

        @pl.when(tm == 0)
        def _():
            def own(b):
                near[W + b, 0:4] = start[:, pl.ds(pl.multiple_of(b * BS, BS), BS)]

            rows_loop(0, rows, own)
            for j in range(edge):
                spread(land[NODES, LEFT, j], near, 4 * j, 0)
                spread(land[NODES, RIGHT, j], near, W + rows + 4 * j, 0)

        @pl.when(tm > 0)
        def _():
            for copy, _, hears in s_copies(it):
                pl.when(hears)(copy.wait_recv)
            for j in range(rows // 4):
                spread(s_land[it, j], near, W + 4 * j, 0)
            for j in range(edge):
                spread(s_halo[it, LEFT, j], near, 4 * j, 0)
                spread(s_halo[it, RIGHT, j], near, W + rows + 4 * j, 0)

        def middle(b):
            own = near[W + b, 0:4]
            change = STEP * react(own, b)
            spread_s = dot(gather(near, b), comp_w[b, 2 * BS :])[:4]
            got = dot(own + change + sum_c[b], comp_w[b, BS : 2 * BS]) + spread_s
            near_q[W + b, 0:4] = got
            partial[b] = 0.5 * spread_s
            state[b] = own + sum_t[b] + 0.5 * change

        rows_loop(0, W, middle)
        rows_loop(rows - W, rows, middle)
        halo_send(MIDDLE, [lambda b: near_q[W + b, 0:4]])
        rows_loop(W, rows - W, middle)

        def local_end(b):
            own, mid = near[W + b, 0:4], near_q[W + b, 0:4]
            right = state[b] + HALF * react(mid, b)
            both = jnp.concatenate([0.5 * (own - mid), right], axis=1)
            partial[b] += dot(both, comp_w[b, : 2 * BS])

        rows_loop(0, rows, local_end)

        def end(b):
            grown[b] = partial[b] + 0.5 * dot(gather(near_q, b), comp_w[b, 2 * BS :])[:4]

        inner, outer = order(end)
        inner()
        halo_wait(MIDDLE, 1)
        halo_place(MIDDLE, near_q, 1)
        outer()

        for j in range(rows // 4):
            tile = jnp.concatenate([grown[4 * j + g] for g in range(4)], axis=0)
            own_send[it, j] = tile.astype(jnp.bfloat16)
        for copy, sends, _ in s_copies(it):
            pl.when(sends)(copy.start)

        def renew(b):
            own = near[W + b, 0:4]
            nodes[b, 0:4] = own
            nodes[b, 4:8] = grown[b]
            mid_b[b] += 0.5 * (own + grown[b])

        rows_loop(0, rows, renew)
        return carry

    lax.fori_loop(0, ITERS, iteration, 0)

    def write(b):
        at = pl.ds(pl.multiple_of(b * BS, BS), BS)
        out[0, 0, :, at] = nodes[b, 0:4]
        out[0, 1, :, at] = mid_b[b]
        out[0, 2, :, at] = nodes[b, 4:8]

    rows_loop(0, rows, write)
    for it in range(ITERS):
        for copy, sends, _ in s_copies(it):
            pl.when(sends)(copy.wait_send)


def shards(n_tm, n_sp, start, guess, diag, off, columns, rates, mixing, fine, coarse):
    rows = diag.shape[0]
    f32, bf16 = jnp.float32, jnp.bfloat16
    vmem = pl.BlockSpec(memory_space=pltpu.VMEM)
    smem = pl.BlockSpec(memory_space=pltpu.SMEM)
    hbm = pl.BlockSpec(memory_space=pl.ANY)
    field = pltpu.VMEM((rows, SPECIES, BS), f32)
    edge = W // 4
    scratch = [
        pltpu.VMEM((rows, BS, BS), bf16), pltpu.VMEM((rows, K, BS, BS), bf16),
        pltpu.VMEM((rows, BS, BS), bf16), pltpu.VMEM((rows, BS, BS), bf16),
        pltpu.VMEM((rows, (K + 1) * BS, BS), bf16), pltpu.VMEM((rows, BS, BS), bf16),
        pltpu.VMEM((rows, (K + 2) * BS, BS), bf16),
        pltpu.VMEM((rows + 2 * W, 8, BS), f32), pltpu.VMEM((rows + 2 * W, 8, BS), f32),
        pltpu.VMEM((SPECIES, 8, BS), f32), pltpu.VMEM((rows, 8, BS), f32),
        *[field] * 11,
        pltpu.VMEM((4, 2, 2 * edge, 16, BS), bf16), pltpu.VMEM((4, 2, 2 * edge, 16, BS), bf16),
        pltpu.VMEM((ITERS, rows // 4, 16, BS), bf16), pltpu.VMEM((ITERS, rows // 4, 16, BS), bf16),
        pltpu.VMEM((ITERS, 2, edge, 16, BS), bf16),
        pltpu.SMEM((rows, K), jnp.int32),
        pltpu.SemaphoreType.DMA((4,)), pltpu.SemaphoreType.DMA((4, 2)), pltpu.SemaphoreType.DMA((4, 2)),
        pltpu.SemaphoreType.DMA((ITERS, 3)), pltpu.SemaphoreType.DMA((ITERS, 3)),
    ]
    return pl.pallas_call(
        functools.partial(kernel, n_tm, n_sp, rows),
        out_shape=jax.ShapeDtypeStruct((1, 3, SPECIES, rows * BS), f32),
        in_specs=[vmem, vmem, smem, vmem, vmem, hbm, hbm, hbm, hbm],
        out_specs=vmem,
        scratch_shapes=scratch,
        compiler_params=pltpu.CompilerParams(
            collective_id=0, has_side_effects=True, vmem_limit_bytes=48 << 20
        ),
    )(start, guess, columns, rates.reshape(rows, BS), mixing, diag, off, fine, coarse)


def solution(mesh):
    in_specs = (
        P(None, "space"),
        P("tm", None, "space"),
        P("space", None, None),
        P("space", None, None, None),
        P("space", None),
        P("space"),
        P(),
        P("space", None, None),
        P("space", None, None),
    )
    out_specs = P("tm", None, None, "space")
    body = functools.partial(shards, mesh.shape["tm"], mesh.shape["space"])
    return jax.shard_map(body, mesh=mesh, in_specs=in_specs, out_specs=out_specs, check_vma=False)
```

time: 1230 us -> 144 us (0.12); the launches traced: 1210 us -> 142 us
  matrix products: 463 us -> 0 us
  starting transfers between devices: 416 us -> 0 us
  waiting for transfers between devices: 228 us -> 0 us
  Pallas kernels: 0 us -> 134 us
  local copies, waits for them, and re-layouts: 79.5 us -> 8.19 us
  other arithmetic: 13.8 us -> 0 us
    dot_general x246 -> x0, matrix products: 463 us -> none  [the longest x68 199 us: apply_inverse(): jnp.einsum('bij,sbj->sbi', inverse_blocks, narrow, preferred_element_type...]
    ppermute x172 -> x0, starting transfers between devices: 416 us -> none  [the longest x70 285 us: extended(): lax.ppermute(tail, axis, [(i, (i + 1) % count) for i in range(ends)])]
    ppermute x172 -> x0, waiting for transfers between devices: 228 us -> none  [the longest x32 210 us: from_behind(): return lax.ppermute(block, axis, route)]
    pallas_call x0 -> x1, Pallas kernels: none -> 134 us  [shards(): pl.pallas_call(functools.partial(kernel, n_tm, n_sp, rows), out_shape=jax...]
    gather x72 -> x0, local copies, waits for them, and re-layouts: 55.4 us -> none  [products(): nearby = jnp.take(widened_blocks, local_columns, axis=2)]
    and x33 -> x0, local copies, waits for them, and re-layouts: 12.8 us -> none  [products(): nearby = jnp.take(widened_blocks, local_columns, axis=2)]
  transfers between devices with their start and end apart: 172 -> 0, of which waited for: 69 -> 0; matrix products, arithmetic and copies ran while one was open for 9% -> 0% of each run, Pallas kernels for 0% -> 0%
where the time goes in v1:
time: 144 us; the launch traced here: 142 us
  Pallas kernels  134 us (93%)
  local copies, waits for them, and re-layouts  8.19 us (6%)
    pallas_call x1, Pallas kernels, shards(): pl.pallas_call(functools.partial(kernel, n_tm, n_sp, rows), out_shape=jax...  134 us
    unnamed x16, local copies, waits for them, and re-layouts  8.19 us

profile of v1, /device:TPU:120, one launch (start us, length us, event | category | flops | bytes accessed | tf_op | source)
XLA Modules:
  0.0 141.8 jit_solution(5821626638004191729)
XLA Ops:
  0.0 0.8 copy.10.cols
  0.8 0.0 copy-start
  0.8 1.2 copy-done
  2.0 0.0 copy-start.1
  2.0 1.2 copy-done.1
  3.2 0.0 copy-start.2
  3.2 1.2 copy-done.2
  4.4 0.0 copy-start.3
  4.4 0.8 copy-done.3
  5.3 0.0 copy-start.4
  5.3 0.8 copy-done.4
  6.1 0.0 copy-start.5
  6.1 0.7 copy-done.5
  6.8 0.0 copy-start.6
  6.8 0.7 copy-done.6
  7.5 133.6 %shard_map.91 = f32[1,3,4,4096]{3,2,1,0:T(4,128)S(1)} custom-call(f32[4,4096]{1,0:T(4,128)S(1)} %copy-done.3, f32[1,4,4096]{2,1,0:T(4,128)S(1)} %copy-done.4, s32[32,4]{1,0:T(8,128)S(1)} %copy.10.cols, f32[32,128]{1,0:T(8,128)S(1)} %bitcast.1, f32[4,4]{1,0:T(4,128)S(1)} %copy-done.6, bf16[32,128,128]{2,1,0:T(8,128)(2,1)S(1)} %copy-done, ...), custom_call_target="tpu_custom_call" | custom-call | tf_op jit(solution)/shard_map/pallas_call | solution.py:399
  141.1 0.7 copy.12
Async XLA Ops:
  0.8 1.2 copy-start
  2.0 1.2 copy-start.1
  3.2 1.2 copy-start.2
  4.4 0.8 copy-start.3
  5.3 0.8 copy-start.4
  6.1 0.7 copy-start.5
  6.8 0.7 copy-start.6

commit v2 on v1

v2 whole, which is shorter than its diff:
```python
import functools

import jax
import jax.numpy as jnp
from jax import lax
from jax.experimental import pallas as pl
from jax.experimental.pallas import tpu as pltpu
from jax.sharding import PartitionSpec as P

BS = 128
K = 4
SPECIES = 4
ITERS = 2
W = 8
STEP = 0.25
HALF = STEP / 2
MESH = pl.DeviceIdType.MESH
NODES, FIRST, SECOND = range(3)
LEFT, RIGHT = 0, 1
GROUP = 4
OWN = 16
WINDOW = OWN + 2 * W
T_OWN, T_WINDOW, T_EDGE = OWN // 4, WINDOW // 4, W // 4


def dot(lhs, rhs):
    return lax.dot_general(
        lhs.astype(jnp.bfloat16), rhs, (((1,), (0,)), ((), ())), preferred_element_type=jnp.float32
    )


def rows_loop(first, last, body):
    def step(i, carry):
        body(i)
        return carry

    lax.fori_loop(first, last, step, 0, unroll=True)


def kernel(
    n_tm, n_sp, rows,
    start_h, guess_h, cols_h, rates_h, mixing_h, diag_h, off_h, fine_h, coarse_h,
    out,
    start, guess, cols, rates, mixing,
    diag_v, off_v, fine_v, raw_w, diag_w, fine_w, win_diag, win_off, win_coarse, win_rates, comp_w, inverse_w,
    near, near_q, mix_v, nodes, imp_b, exp_b, mid_b, first_v, second_r,
    sum_c, sum_t, state, solved, partial, fresh, right_v,
    send_b, land, terms_b, terms_land, rest_land, start_b, chain_land, end_b, value_land, value_halo,
    cols_land, cols_s, place_of, place_w,
    load_sem, send_sem, recv_sem, unit_send, unit_recv, cols_send, cols_recv,
    terms_send, terms_recv, start_send, chain_send, chain_recv, value_send, value_recv,
):
    tm = lax.axis_index("tm")
    sp = lax.axis_index("space")
    plane, line, chip, core = tm // GROUP, tm % GROUP, sp // 2, sp % 2
    has_left, has_right = sp > 0, sp < n_sp - 1
    edge = W // 4
    chunks = n_sp * rows // OWN

    def quarter(x, y):
        return jnp.where(x % 2 == 0, y, GROUP - 1 - y)

    def chain_device(i, z):
        x, j = i // GROUP, i % GROUP
        return z * GROUP + quarter(x, j), 2 * x + 1

    def chain_plane(group):
        return (group + 2) % GROUP

    mine = quarter(chip, line)
    chunk = GROUP * chip + mine
    group = (plane + 2) % GROUP
    on_chain = core == 1
    even = chunk % 2 == 0
    chunk_left, chunk_right = chunk > 0, chunk < chunks - 1
    owner = chunk // 2
    beside = jnp.where(even, owner - 1, owner + 1)
    has_beside = (even & chunk_left) | (~even & chunk_right)
    low, high = 2 * sp, 2 * sp + 1

    def remote(src, dst, out_sem, in_sem, device):
        return pltpu.make_async_remote_copy(
            src_ref=src, dst_ref=dst, send_sem=out_sem, recv_sem=in_sem,
            device_id=device, device_id_type=MESH,
        )

    def arrive(dst, in_sem, there=None):
        def wait():
            remote(dst, dst, send_sem.at[0, 0], in_sem, (tm, sp)).wait_recv()

        if there is None:
            wait()
        else:
            pl.when(there)(wait)

    loads = [
        pltpu.make_async_copy(src, dst, load_sem.at[i])
        for i, (src, dst) in enumerate((
            (mixing_h, mixing), (guess_h, guess), (start_h, start), (cols_h, cols), (rates_h, rates),
            (diag_h, diag_v), (off_h, off_v), (fine_h, fine_v),
        ))
    ]
    for load in loads:
        load.start()
    small, large = loads[:5], loads[5:]
    cols_land[...] = jnp.zeros_like(cols_land)

    barrier = pltpu.get_barrier_semaphore()
    my_plane = chain_plane(plane)
    later, before = group < GROUP - 1, group > 0
    after, earlier = (plane + 1) % GROUP, (plane + GROUP - 1) % GROUP
    senders, receivers = [], []

    def both(device, there):
        senders.append((device, there))
        receivers.append(there)

    both((tm, sp - 1), has_left)
    both((tm, sp + 1), has_right)
    for i, there in ((low - 1, has_left), (low, True), (high, True), (high + 1, has_right)):
        both(chain_device(i, my_plane), there)
        senders.append((chain_device(i, chain_plane(plane + GROUP - 1)), there & (line == 0) & (plane > 0)))
    for y in range(GROUP):
        both((group * GROUP + y, owner), on_chain)
        both((group * GROUP + y, beside), on_chain & has_beside)
    receivers.append(on_chain & later)
    receivers.append(on_chain & later & has_beside)
    both(chain_device(chunk - 1, plane), on_chain & chunk_left)
    both(chain_device(chunk + 1, plane), on_chain & chunk_right)
    for i, there in ((chunk, True), (chunk - 1, chunk_left), (chunk + 1, chunk_right)):
        senders.append((chain_device(i, earlier), on_chain & before & there))
        receivers.append(on_chain & later & there)

    for device, there in senders:
        def signal(device=device):
            pl.semaphore_signal(barrier, inc=1, device_id=device, device_id_type=MESH)

        pl.when(there)(signal)

    for load in small:
        load.wait()

    def local_place(b, carry):
        for k in range(K):
            place_of[b, k] = jnp.clip(cols[0, b * K + k] - (sp * rows - W), 0, rows + 2 * W - 1)
        return carry

    lax.fori_loop(0, rows, local_place, 0)
    near[...] = jnp.zeros_like(near)
    near_q[...] = jnp.zeros_like(near_q)
    imp_b[...] = jnp.zeros_like(imp_b)
    exp_b[...] = jnp.zeros_like(exp_b)
    for t in range(SPECIES):
        column = jnp.broadcast_to(mixing[:, t : t + 1], (SPECIES, BS))
        mix_v[t] = jnp.concatenate([column, column], axis=0)

    def cells(b):
        return pl.ds(pl.multiple_of(b * BS, BS), BS)

    def begin(b):
        own = guess[0, :, cells(b)]
        nodes[b, 0:4] = jnp.where(tm == 0, start[:, cells(b)], own)
        nodes[b, 4:8] = own

    rows_loop(0, rows, begin)

    pl.semaphore_wait(barrier, sum(jnp.asarray(there).astype(jnp.int32) for there in receivers))

    def unit_copies(unit, at, device, extra=0):
        src, dst = pl.ds(unit * W, W), pl.ds(pl.multiple_of(at * W, W), W)
        pairs = ((off_h, win_off), (coarse_h, win_coarse), (rates_h, win_rates), (diag_h, win_diag))
        copies = []
        for n, (a, b) in enumerate(pairs):
            if device is None:
                copies.append(pltpu.make_async_copy(a.at[src], b.at[dst], unit_recv.at[at, n]))
            else:
                copies.append(remote(a.at[src], b.at[dst], unit_send.at[4 if extra else unit, n], unit_recv.at[at, n], device))
        return copies

    def unit_plan():
        plan = []
        for unit in range(4):
            at = unit - 2 * mine + 1
            plan.append((unit, at, (tm, sp + 1), (core == 0) & (at >= 0) & (at < 4), 0))
            at = unit + 4 - 2 * mine + 1
            plan.append((unit, at, None, on_chain & (at >= 0) & (at < 4), 0))
        next_low = quarter(chip + 1, line) == 0
        plan.append((3, 0, (tm, sp + 2), on_chain & (chip < n_sp // 2 - 1) & next_low, 1))
        last_high = quarter(chip - 1, line) == GROUP - 1
        plan.append((0, 3, (tm, sp - 1), (core == 0) & (chip > 0) & last_high, 1))
        return plan

    def cols_copy(which):
        slot, device = ((1, (tm, sp + 1)), (3, (tm, sp - 1)), (0, (tm, sp + 2)))[which]
        return remote(cols_h, cols_land.at[slot], cols_send.at[which], cols_recv.at[slot], device)

    def cols_plan():
        next_low = quarter(chip + 1, line) == 0
        last_high = quarter(chip - 1, line) == GROUP - 1
        return (
            (0, core == 0),
            (1, (core == 0) & (chip > 0) & last_high),
            (2, on_chain & (chip < n_sp // 2 - 1) & next_low),
        )

    def weights_out():
        for which, there in cols_plan():
            pl.when(there)(cols_copy(which).start)
        for unit, at, device, there, extra in unit_plan():
            def go(unit=unit, at=at, device=device, extra=extra):
                copies = unit_copies(unit, at, device, extra)
                for copy in copies[:3]:
                    copy.start()
                pl.when((at == 1) | (at == 2))(copies[3].start)

            pl.when(there)(go)

    def weights_sent():
        for which, there in cols_plan():
            pl.when(there)(cols_copy(which).wait_send)
        for unit, at, device, there, extra in unit_plan():
            if device is None:
                continue

            def done(unit=unit, at=at, device=device, extra=extra):
                copies = unit_copies(unit, at, device, extra)
                for copy in copies[:3]:
                    copy.wait_send()
                pl.when((at == 1) | (at == 2))(copies[3].wait_send)

            pl.when(there)(done)

    pl.when(plane == chain_plane(0))(weights_out)

    def halo_copies(kind, count):
        to_left = remote(
            send_b.at[kind, LEFT, pl.ds(0, count)], land.at[kind, RIGHT, pl.ds(0, count)],
            send_sem.at[kind, LEFT], recv_sem.at[kind, RIGHT], (tm, sp - 1),
        )
        to_right = remote(
            send_b.at[kind, RIGHT, pl.ds(0, count)], land.at[kind, LEFT, pl.ds(0, count)],
            send_sem.at[kind, RIGHT], recv_sem.at[kind, LEFT], (tm, sp + 1),
        )
        return to_left, to_right

    def tile(values):
        return jnp.concatenate(values, axis=0).astype(jnp.bfloat16)

    def halo_send(kind, fields):
        for f, field in enumerate(fields):
            for j in range(edge):
                send_b[kind, LEFT, f * edge + j] = tile([field(4 * j + g) for g in range(4)])
                send_b[kind, RIGHT, f * edge + j] = tile([field(rows - W + 4 * j + g) for g in range(4)])
        to_left, to_right = halo_copies(kind, edge * len(fields))
        pl.when(has_left)(to_left.start)
        pl.when(has_right)(to_right.start)

    def halo_wait(kind, count):
        to_left, to_right = halo_copies(kind, edge * count)

        @pl.when(has_left)
        def _():
            to_right.wait_recv()
            to_left.wait_send()

        @pl.when(has_right)
        def _():
            to_left.wait_recv()
            to_right.wait_send()

    def spread(block_tile, target, block, row):
        wide = block_tile.astype(jnp.float32)
        for g in range(4):
            target[block + g, row : row + 4] = wide[4 * g : 4 * g + 4]

    def halo_place(kind, target, count):
        for f in range(count):
            for j in range(edge):
                spread(land[kind, LEFT, f * edge + j], target, 4 * j, 4 * f)
                spread(land[kind, RIGHT, f * edge + j], target, W + rows + 4 * j, 4 * f)

    def gather(source, places, b):
        return jnp.concatenate([source[places[b, k]] for k in range(K)], axis=1)

    def react(v, rate):
        total = None
        for t in range(SPECIES):
            line_t = v[t : t + 1]
            if v.shape[0] == 8:
                second = v[4 + t : 5 + t]
                row = lax.broadcasted_iota(jnp.int32, (8, BS), 0)
                line_t = jnp.where(row < 4, jnp.broadcast_to(line_t, (8, BS)), jnp.broadcast_to(second, (8, BS)))
            term = mix_v[t, : v.shape[0]] * line_t
            total = term if total is None else total + term
        return total * rate

    def paired(first, second, weights):
        got = dot(jnp.concatenate([first, second], axis=0), weights)
        return got[:8, :BS], got[8:, BS:]

    def explicit(b, count):
        got = dot(gather(near, place_of, b), raw_w[b])[: 4 * count]
        return got + react(near[W + b, : 4 * count], rates[pl.ds(b, 1)])

    def transposed(n, carry):
        for r in range(4):
            b, half = 4 * n + r, pl.ds(BS * (r % 2), BS)
            diag_w[2 * n + r // 2, :, half] = diag_v[b].T
            fine_w[2 * n + r // 2, :, half] = fine_v[b].T
            for k in range(K):
                raw_w[b, BS * k : BS * (k + 1)] = off_v[b, k].T
        return carry

    def outer(*bodies):
        for body in bodies:
            rows_loop(0, W // 2, body)
            rows_loop((rows - W) // 2, rows // 2, body)

    def inner(*bodies):
        for body in bodies:
            rows_loop(W // 2, (rows - W) // 2, body)

    def solve(target):
        def pair(i):
            got = paired(right_v[2 * i], right_v[2 * i + 1], fine_w[i])
            target[2 * i], target[2 * i + 1] = got[0][:4], got[1][:4]

        return pair

    def terms_copies(it):
        slot = it * GROUP + line
        main, rest = terms_land.at[slot], rest_land.at[slot]
        to = [chain_device(i, my_plane) for i in (low, high, low - 1, high + 1)]

        def piece(first, count, dst, n, sem, device):
            return remote(
                terms_b.at[it, pl.ds(first, count)], dst, terms_send.at[it, n], terms_recv.at[slot, sem], device
            )

        t_rows = rows // 4
        return (
            (piece(0, 6, main.at[pl.ds(2, 6)], 0, 0, to[0]), True),
            (piece(2, 6, main.at[pl.ds(0, 6)], 1, 0, to[1]), True),
            (piece(0, 2, main.at[pl.ds(6, 2)], 2, 1, to[2]), has_left),
            (piece(6, 2, main.at[pl.ds(0, 2)], 3, 1, to[3]), has_right),
            (piece(t_rows, T_OWN, rest, 4, 2, to[0]), True),
            (piece(t_rows + T_OWN, T_OWN, rest, 5, 2, to[1]), True),
        )

    def fine(it):
        @pl.when(it == 0)
        def _():
            halo_send(NODES, [lambda b: nodes[b, 0:4], lambda b: nodes[b, 4:8]])
            for load in large:
                load.wait()
            lax.fori_loop(0, rows // 4, transposed, 0)
            halo_wait(NODES, 2)
            halo_place(NODES, near, 2)

        @pl.when(it == 1)
        def _():
            @pl.when(tm > 0)
            def _():
                values_wait(0, 0, True)
                for j in range(rows // 4):
                    spread(value_land[0, 0, j], nodes, 4 * j, 0)
                for j in range(edge):
                    spread(value_halo[0, LEFT, j], near, 4 * j, 0)
                    spread(value_halo[0, RIGHT, j], near, W + rows + 4 * j, 0)

            @pl.when(tm == 0)
            def _():
                for j in range(edge):
                    spread(land[NODES, LEFT, j], near, 4 * j, 0)
                    spread(land[NODES, RIGHT, j], near, W + rows + 4 * j, 0)

            values_wait(0, 1, True)
            for j in range(rows // 4):
                spread(value_land[0, 1, j], nodes, 4 * j, 4)
            for j in range(edge):
                spread(value_halo[1, LEFT, j], near, 4 * j, 4)
                spread(value_halo[1, RIGHT, j], near, W + rows + 4 * j, 4)

        def place(b):
            near[W + b] = nodes[b]

        rows_loop(0, rows, place)
        own_part = jnp.where(it == 0, 0.0, 0.5)
        end_part = jnp.where(it == 0, 1.0, 0.5)

        def node_terms(i):
            imps = paired(near[W + 2 * i], near[W + 2 * i + 1], diag_w[i])
            for b, imp in zip((2 * i, 2 * i + 1), imps):
                exp = explicit(b, 2)
                imp_0, exp_0, imp_2, exp_2 = imp[:4], exp[:4], imp[4:], exp[4:]
                one_i = imp_b[b] + own_part * imp_0 + end_part * imp_2
                one_e = exp_b[b] + own_part * exp_0 + end_part * exp_2
                f_0, f_1, f_2 = imp_0 + exp_0, one_i + one_e, imp_2 + exp_2
                right_v[b, 0:4] = (
                    nodes[b, 0:4] - HALF * one_i + STEP * (5 / 24 * f_0 + 1 / 3 * f_1 - 1 / 24 * f_2)
                )
                second_r[b] = STEP * (-1 / 24 * f_0 + 1 / 3 * f_1 + 5 / 24 * f_2) - HALF * (one_e + imp_2)
                sum_c[b] = STEP * (1 / 6 * f_0 - exp_0)
                sum_t[b] = (-STEP / 3) * f_0
                imp_b[b] = -0.5 * imp_0
                exp_b[b] = -0.5 * exp_0

        outer(node_terms, solve(first_v))
        halo_send(FIRST, [lambda b: first_v[b]])
        inner(node_terms, solve(first_v))

        def put_first(b):
            near[W + b, 0:4] = first_v[b]

        rows_loop(0, rows, put_first)
        halo_wait(FIRST, 1)
        halo_place(FIRST, near, 1)

        def first_terms(i):
            imps = paired(near[W + 2 * i], near[W + 2 * i + 1], diag_w[i])
            for b, imp in zip((2 * i, 2 * i + 1), imps):
                imp = imp[:4]
                exp = explicit(b, 1)
                force = STEP * 2 / 3 * (imp + exp)
                right_v[b, 0:4] = first_v[b] + HALF * exp + second_r[b]
                sum_c[b] += force
                sum_t[b] += force
                imp_b[b] += imp
                exp_b[b] += exp

        outer(first_terms, solve(fresh))
        halo_send(SECOND, [lambda b: fresh[b]])
        inner(first_terms, solve(fresh))

        def put_second(b):
            near[W + b, 0:4] = fresh[b]
            mid_b[b] = first_v[b] - 0.5 * (nodes[b, 0:4] + fresh[b])

        rows_loop(0, rows, put_second)

        def second_terms(i):
            imps = paired(near[W + 2 * i], near[W + 2 * i + 1], diag_w[i])
            for b, imp in zip((2 * i, 2 * i + 1), imps):
                imp = imp[:4]
                exp = explicit(b, 1)
                force = imp + exp
                sum_c[b] += STEP * (1 / 6 * force - imp)
                sum_t[b] += (-STEP / 3) * force
                imp_b[b] += -0.5 * imp
                exp_b[b] += -0.5 * exp

        inner(second_terms)
        halo_wait(SECOND, 1)
        halo_place(SECOND, near, 1)
        outer(second_terms)
        for j in range(rows // 4):
            terms_b[it, j] = tile([sum_c[4 * j + g] for g in range(4)])
            terms_b[it, rows // 4 + j] = tile([sum_t[4 * j + g] for g in range(4)])
        for copy, there in terms_copies(it):
            if there is True:
                copy.start()
            else:
                pl.when(there)(copy.start)

    def values_wait(it, which, halos):
        for n in range(2):
            arrive(value_land.at[it, which, pl.ds(n * T_OWN, T_OWN)], value_recv.at[it, which, n])
        if halos:
            arrive(value_halo.at[which, LEFT], value_recv.at[it, which, 2], has_left)
            arrive(value_halo.at[which, RIGHT], value_recv.at[it, which, 3], has_right)

    def value_copies(it, j):
        g = it * GROUP + j
        p = group * GROUP + j
        half = chunk % 2
        copies = []
        for which in (1, 0):
            t = p + 1 - which
            there = (p < n_tm - 1) if which == 0 else True
            copies.append((remote(
                end_b.at[g], value_land.at[it, which, pl.ds(pl.multiple_of(half * T_OWN, T_OWN), T_OWN)],
                value_send.at[g, which, 0], value_recv.at[it, which, half], (t, owner)), there))
            copies.append((remote(
                end_b.at[g, pl.ds(pl.multiple_of(half * (T_OWN - T_EDGE), T_EDGE), T_EDGE)], value_halo.at[which, 1 - half],
                value_send.at[g, which, 1], value_recv.at[it, which, 3 - half], (t, beside)),
                there & has_beside & (it == 0)))
        return copies

    def chain_copies(it, j):
        g = it * GROUP + j
        inside = j < GROUP - 1
        target = jnp.where(inside, g + 1, it * GROUP)
        z = jnp.where(inside, plane, after)
        there = inside | later
        copies = []
        for n, (i, ok) in enumerate(((chunk - 1, chunk_left), (chunk, ~inside), (chunk + 1, chunk_right))):
            part = 2 - n
            copies.append((remote(
                end_b.at[g], chain_land.at[target, part], chain_send.at[g, n], chain_recv.at[target, part],
                chain_device(i, z)), there & ok))
        return copies

    def start_copies():
        copies = []
        for n, (i, part, half, ok) in enumerate((
            (low, 1, 0, True), (low, 2, 1, True), (low - 1, 2, 0, has_left),
            (high, 1, 1, True), (high, 0, 0, True), (high + 1, 0, 1, has_right),
        )):
            copies.append((remote(
                start_b.at[pl.ds(half * T_OWN, T_OWN)], chain_land.at[0, part], start_send.at[n],
                chain_recv.at[0, part], chain_device(i, chain_plane(0))), (tm == 0) & ok))
        return copies

    @pl.when(tm == 0)
    def _():
        for j in range(rows // 4):
            start_b[j] = tile([nodes[4 * j + g, 0:4] for g in range(4)])
        for copy, there in start_copies():
            pl.when(there)(copy.start)

    def window_weights():
        first_unit = 2 * mine - 1
        arrive(cols_land.at[1], cols_recv.at[1])
        arrive(cols_land.at[0], cols_recv.at[0], (mine == 0) & (chip > 0))
        arrive(cols_land.at[3], cols_recv.at[3], (mine == GROUP - 1) & (chip < n_sp // 2 - 1))
        to_scalars = pltpu.make_async_copy(cols_land, cols_s, cols_send.at[3])
        to_scalars.start()
        for at in range(4):
            there = (first_unit + at >= 0) | (chip > 0)
            there = there & ((first_unit + at < 8) | (chip < n_sp // 2 - 1))

            @pl.when(there)
            def _(at=at):
                copies = unit_copies(0, at, (tm, sp))
                for copy in copies[:3] if at in (0, 3) else copies:
                    copy.wait_recv()

        to_scalars.wait()

        def places(w, carry):
            unit = first_unit + w // W
            slot, row = (unit + 4) // 4, (unit + 4) % 4 * W + w % W
            for k in range(K):
                column = jnp.where(slot == 2, cols[0, row * K + k], cols_s[slot, 0, row * K + k])
                place_w[w, k] = jnp.clip(column - (chunk * OWN - 2 * W), 0, OWN + 4 * W - 1)
            return carry

        lax.fori_loop(0, WINDOW, places, 0)

        def composed(n, carry):
            for r in range(4):
                w = 4 * n + r
                inverse = win_coarse[w].T
                comp_w[w, BS : 2 * BS] = inverse
                inverse_w[2 * n + r // 2, :, BS * (r % 2) : BS * (r % 2 + 1)] = inverse
                raw = [win_diag[w]] + [win_off[w, k] for k in range(K)]
                got = (dot(jnp.concatenate([block.T for block in raw], axis=0), inverse) * STEP).astype(jnp.bfloat16)
                comp_w[w, :BS] = got[:BS]
                comp_w[w, 2 * BS :] = got[BS:]
            return carry

        lax.fori_loop(0, WINDOW // 4, composed, 0)

    def chain_step(g, carry):
        it, j = g // GROUP, g % GROUP
        from_start = (j == 0) & (group == 0)
        slot = jnp.where(from_start, 0, g)

        fresh_start = ~(from_start & (it == 1))
        main_at = jnp.where(even, 2, 0)
        halo_at = jnp.where(even, 0, 6)

        @pl.when(j == 0)
        def _():
            arrive(chain_land.at[g, 1], chain_recv.at[g, 1], fresh_start)
            for n in range(T_OWN):
                spread(chain_land[slot, 1, n], near, 2 * W + 4 * n, 0)

        arrive(terms_land.at[g, pl.ds(main_at, 6)], terms_recv.at[g, 0])
        arrive(terms_land.at[g, pl.ds(halo_at, 2)], terms_recv.at[g, 1], has_beside)
        arrive(rest_land.at[g], terms_recv.at[g, 2])

        def prepare(n):
            constant = terms_land[g, n].astype(jnp.float32)
            for r in range(4):
                w = 4 * n + r
                own = near[W + w, 0:4]
                change = STEP * react(own, win_rates[pl.ds(w, 1)])
                right_v[w, 0:4] = own + change + constant[4 * r : 4 * r + 4]
                state[w] = own + 0.5 * change
            for i in (2 * n, 2 * n + 1):
                got = paired(right_v[2 * i], right_v[2 * i + 1], inverse_w[i])
                solved[2 * i], solved[2 * i + 1] = got[0][:4], got[1][:4]

        rows_loop(T_EDGE, T_WINDOW - T_EDGE, prepare)

        def with_rest(n):
            constant = rest_land[g, n].astype(jnp.float32)
            for r in range(4):
                state[W + 4 * n + r] += constant[4 * r : 4 * r + 4]

        rows_loop(0, T_OWN, with_rest)

        @pl.when(fresh_start)
        def _():
            arrive(chain_land.at[g, 0], chain_recv.at[g, 0], chunk_left)
            arrive(chain_land.at[g, 2], chain_recv.at[g, 2], chunk_right)

        for n in range(T_OWN):
            spread(chain_land[slot, 0, n], near, 4 * n, 0)
            spread(chain_land[slot, 2, n], near, 2 * W + OWN + 4 * n, 0)

        rows_loop(0, T_EDGE, prepare)
        rows_loop(T_WINDOW - T_EDGE, T_WINDOW, prepare)

        def middle(w):
            spread_s = dot(gather(near, place_w, w), comp_w[w, 2 * BS :])[:4]
            near_q[W + w, 0:4] = solved[w] + spread_s
            partial[w] = 0.5 * spread_s

        rows_loop(0, WINDOW, middle)

        def end(o):
            w = W + o
            own, mid = near[W + w, 0:4], near_q[W + w, 0:4]
            right = state[w] + HALF * react(mid, win_rates[pl.ds(w, 1)])
            parts = jnp.concatenate([0.5 * (own - mid), right, 0.5 * gather(near_q, place_w, w)[:4]], axis=1)
            near[W + w, 0:4] = partial[w] + dot(parts, comp_w[w])

        rows_loop(0, OWN, end)
        for n in range(T_OWN):
            end_b[g, n] = tile([near[2 * W + 4 * n + r, 0:4] for r in range(4)])
        for copy, there in chain_copies(it, j):
            pl.when(there)(copy.start)
        for copy, there in value_copies(it, j):
            if there is True:
                copy.start()
            else:
                pl.when(there)(copy.start)
        return carry

    def round_of(it, carry):
        fine(it)
        pl.when((it == 0) & (plane != chain_plane(0)))(weights_out)

        @pl.when(on_chain & ((group < 2) == (it == 0)))
        def _():
            window_weights()
            lax.fori_loop(0, ITERS * GROUP, chain_step, 0)

        return carry

    lax.fori_loop(0, ITERS, round_of, 0)

    pl.when(tm > 0)(lambda: values_wait(1, 0, False))
    values_wait(1, 1, False)

    def write(j):
        ends = value_land[1, 1, j].astype(jnp.float32)
        starts = value_land[1, 0, j].astype(jnp.float32)
        for g in range(4):
            b = 4 * j + g
            own = jnp.where(tm == 0, start[:, cells(b)], starts[4 * g : 4 * g + 4])
            last = ends[4 * g : 4 * g + 4]
            out[0, 0, :, cells(b)] = own
            out[0, 1, :, cells(b)] = mid_b[b] + 0.5 * (own + last)
            out[0, 2, :, cells(b)] = last

    rows_loop(0, rows // 4, write)

    weights_sent()
    for copy, there in start_copies():
        pl.when(there)(copy.wait_send)
    for it in range(ITERS):
        for copy, there in terms_copies(it):
            if there is True:
                copy.wait_send()
            else:
                pl.when(there)(copy.wait_send)

    @pl.when(on_chain)
    def _():
        def sent(g, carry):
            it, j = g // GROUP, g % GROUP
            for copy, there in chain_copies(it, j) + value_copies(it, j):
                if there is True:
                    copy.wait_send()
                else:
                    pl.when(there)(copy.wait_send)
            return carry

        lax.fori_loop(0, ITERS * GROUP, sent, 0)


def shards(n_tm, n_sp, start, guess, diag, off, columns, rates, mixing, fine, coarse):
    rows = diag.shape[0]
    f32, bf16 = jnp.float32, jnp.bfloat16
    vmem = pl.BlockSpec(memory_space=pltpu.VMEM)
    hbm = pl.BlockSpec(memory_space=pltpu.HBM)
    dma = pltpu.SemaphoreType.DMA
    edge = W // 4
    slots = ITERS * GROUP

    def tiles(*lead):
        return pltpu.VMEM((*lead, 16, BS), bf16)

    def blocks(*lead):
        return pltpu.VMEM((*lead, BS, BS), bf16)

    pairs = pltpu.VMEM((rows // 2, BS, 2 * BS), bf16)
    scratch = [
        pltpu.VMEM((SPECIES, rows * BS), f32), pltpu.VMEM((1, SPECIES, rows * BS), f32),
        pltpu.SMEM((1, rows * K), jnp.int32), pltpu.VMEM((rows, BS), f32), pltpu.VMEM((SPECIES, SPECIES), f32),
        blocks(rows), blocks(rows, K), blocks(rows),
        pltpu.VMEM((rows, K * BS, BS), bf16), pairs, pairs,
        blocks(WINDOW), blocks(WINDOW, K), blocks(WINDOW), pltpu.VMEM((WINDOW, BS), f32),
        pltpu.VMEM((WINDOW, (K + 2) * BS, BS), bf16),
        pltpu.VMEM((WINDOW // 2, BS, 2 * BS), bf16),
        pltpu.VMEM((rows + 2 * W, 8, BS), f32), pltpu.VMEM((rows + 2 * W, 8, BS), f32),
        pltpu.VMEM((SPECIES, 8, BS), f32), pltpu.VMEM((rows, 8, BS), f32),
        *[pltpu.VMEM((rows, SPECIES, BS), f32)] * 11, pltpu.VMEM((rows, 8, BS), f32),
        tiles(3, 2, 2 * edge), tiles(3, 2, 2 * edge),
        tiles(ITERS, rows // 2), tiles(slots, T_WINDOW), tiles(slots, T_OWN),
        tiles(rows // 4), tiles(slots, 3, T_OWN), tiles(slots, T_OWN),
        tiles(ITERS, 2, rows // 4), tiles(2, 2, edge),
        pltpu.VMEM((4, 1, BS), jnp.int32), pltpu.SMEM((4, 1, BS), jnp.int32),
        pltpu.SMEM((rows, K), jnp.int32), pltpu.SMEM((WINDOW, K), jnp.int32),
        dma((8,)), dma((3, 2)), dma((3, 2)), dma((5, 4)), dma((4, 4)), dma((4,)), dma((4,)),
        dma((ITERS, 6)), dma((slots, 3)), dma((6,)), dma((slots, 3)), dma((slots, 3)),
        dma((slots, 2, 2)), dma((ITERS, 2, 4)),
    ]
    return pl.pallas_call(
        functools.partial(kernel, n_tm, n_sp, rows),
        out_shape=jax.ShapeDtypeStruct((1, 3, SPECIES, rows * BS), f32),
        in_specs=[hbm] * 9,
        out_specs=vmem,
        scratch_shapes=scratch,
        compiler_params=pltpu.CompilerParams(
            collective_id=0, has_side_effects=True, vmem_limit_bytes=48 << 20
        ),
    )(start, guess, columns.reshape(1, rows * K), rates.reshape(rows, BS), mixing, diag, off, fine, coarse)


def solution(mesh):
    in_specs = (
        P(None, "space"),
        P("tm", None, "space"),
        P("space", None, None),
        P("space", None, None, None),
        P("space", None),
        P("space"),
        P(),
        P("space", None, None),
        P("space", None, None),
    )
    out_specs = P("tm", None, None, "space")
    body = functools.partial(shards, mesh.shape["tm"], mesh.shape["space"])
    return jax.shard_map(body, mesh=mesh, in_specs=in_specs, out_specs=out_specs, check_vma=False)
```

time: 144 us -> 116 us (0.81); the launches traced: 142 us -> 115 us
  Pallas kernels: 134 us -> 107 us
    pallas_call x1, Pallas kernels: 134 us -> 107 us  [shards(): pl.pallas_call(functools.partial(kernel, n_tm, n_sp, rows), out_shape=jax...]
where the time goes in v2:
time: 116 us; the launch traced here: 115 us
  Pallas kernels  107 us (92%)
  local copies, waits for them, and re-layouts  8.29 us (7%)
    pallas_call x1, Pallas kernels, shards(): pl.pallas_call(functools.partial(kernel, n_tm, n_sp, rows), out_shape=jax...  107 us
    unnamed x16, local copies, waits for them, and re-layouts  8.19 us

profile of v2, /device:TPU:120, one launch (start us, length us, event | category | flops | bytes accessed | tf_op | source)
XLA Modules:
  0.0 115.3 jit_solution(9638546424842820944)
XLA Ops:
  0.0 0.8 copy.11
  0.8 0.1 reshape.6.cols_h
  0.9 0.0 copy-start
  0.9 1.2 %copy-done = bf16[32,128,128]{2,1,0:T(8,128)(2,1)S(1)} copy-done((bf16[32,128,128]{2,1,0:T(8,128)(2,1)S(1)}, bf16[32,128,128]{2,1,0:T(8,128)(2,1)}, u32[]{:S(2)}) %copy-start) | copy-done | bytes 1048600
  2.1 0.0 copy-start.1
  2.1 1.2 %copy-done.1 = bf16[32,128,128]{2,1,0:T(8,128)(2,1)S(1)} copy-done((bf16[32,128,128]{2,1,0:T(8,128)(2,1)S(1)}, bf16[32,128,128]{2,1,0:T(8,128)(2,1)}, u32[]{:S(2)}) %copy-start.1) | copy-done | bytes 1048600
  3.3 0.0 copy-start.2
  3.3 1.2 %copy-done.2 = bf16[32,128,128]{2,1,0:T(8,128)(2,1)S(1)} copy-done((bf16[32,128,128]{2,1,0:T(8,128)(2,1)S(1)}, bf16[32,128,128]{2,1,0:T(8,128)(2,1)}, u32[]{:S(2)}) %copy-start.2) | copy-done | bytes 1048600
  4.5 0.0 copy-start.3
  4.6 0.8 copy-done.3
  5.4 0.0 copy-start.4
  5.4 0.8 copy-done.4
  6.2 0.0 copy-start.5
  6.2 0.7 copy-done.5
  6.9 0.0 copy-start.6
  6.9 0.7 copy-done.6
  7.6 106.9 %shard_map.91 = f32[1,3,4,4096]{3,2,1,0:T(4,128)S(1)} custom-call(f32[4,4096]{1,0:T(4,128)S(1)} %copy-done.3, f32[1,4,4096]{2,1,0:T(4,128)S(1)} %copy-done.4, s32[1,128]{1,0:T(1,128)S(1)} %reshape.6.cols_h, f32[32,128]{1,0:T(8,128)S(1)} %bitcast.1, f32[4,4]{1,0:T(4,128)S(1)} %copy-done.6, bf16[32,128,128]{2,1,0:T(8,128)(2,1)S(1)} %copy-done, ...), custom_call_target="tpu_custom_call" | custom-call | tf_op jit(solution)/shard_map/pallas_call | solution.py:732
  114.6 0.7 copy.13
Async XLA Ops:
  0.9 1.2 %copy-start = (bf16[32,128,128]{2,1,0:T(8,128)(2,1)S(1)}, bf16[32,128,128]{2,1,0:T(8,128)(2,1)}, u32[]{:S(2)}) copy-start(bf16[32,128,128]{2,1,0:T(8,128)(2,1)} %diag_h.1) | copy-start | bytes 3145732
  2.1 1.2 %copy-start.1 = (bf16[32,128,128]{2,1,0:T(8,128)(2,1)S(1)}, bf16[32,128,128]{2,1,0:T(8,128)(2,1)}, u32[]{:S(2)}) copy-start(bf16[32,128,128]{2,1,0:T(8,128)(2,1)} %fine_h.1) | copy-start | bytes 3145732
  3.3 1.2 %copy-start.2 = (bf16[32,128,128]{2,1,0:T(8,128)(2,1)S(1)}, bf16[32,128,128]{2,1,0:T(8,128)(2,1)}, u32[]{:S(2)}) copy-start(bf16[32,128,128]{2,1,0:T(8,128)(2,1)} %coarse_h.1) | copy-start | bytes 3145732
  4.5 0.8 copy-start.3
  5.4 0.8 copy-start.4
  6.2 0.7 copy-start.5
  6.9 0.7 copy-start.6

commit v3 on v2

--- a/solution.py
+++ b/solution.py
@@ -21,6 +21,7 @@
 OWN = 16
 WINDOW = OWN + 2 * W
 T_OWN, T_WINDOW, T_EDGE = OWN // 4, WINDOW // 4, W // 4
+PIECES = ((0, 0, 0, 1), (0, 1, 1, 2), (0, GROUP - 1, 3, 1), (1, 0, 4, 2), (GROUP - 1, 0, 6, 2))
 
 
 def dot(lhs, rhs):
@@ -47,7 +48,7 @@
     sum_c, sum_t, state, solved, partial, fresh, right_v,
     send_b, land, terms_b, terms_land, rest_land, start_b, chain_land, end_b, value_land, value_halo,
     cols_land, cols_s, place_of, place_w,
-    load_sem, send_sem, recv_sem, unit_send, unit_recv, cols_send, cols_recv,
+    load_sem, send_sem, recv_sem, unit_send, unit_recv, cols_send, cols_recv, piece_send, piece_recv,
     terms_send, terms_recv, start_send, chain_send, chain_recv, value_send, value_recv,
 ):
     tm = lax.axis_index("tm")
@@ -131,6 +132,29 @@
         senders.append((chain_device(i, earlier), on_chain & before & there))
         receivers.append(on_chain & later & there)
 
+    first_plane = chain_plane(0)
+    lower = on_chain & (mine == 0) & (chip > 0)
+    upper = on_chain & (mine == GROUP - 1) & (chip < n_sp // 2 - 1)
+
+    def piece_sources(n):
+        z = jnp.where(plane == first_plane, (plane + PIECES[n][0]) % GROUP, plane)
+        t = z * GROUP + (line + PIECES[n][1]) % GROUP
+        return ((t, sp - 2), lower), ((t, sp + 1), upper)
+
+    def piece_targets(n, early):
+        z = (plane + GROUP - PIECES[n][0]) % GROUP if early else plane
+        y = (line + GROUP - PIECES[n][1]) % GROUP
+        t = z * GROUP + y
+        fits = (z == first_plane) if early else (z != first_plane)
+        right = on_chain & (chip < n_sp // 2 - 1) & (quarter(chip + 1, y) == 0)
+        left = ~on_chain & (chip > 0) & (quarter(chip - 1, y) == GROUP - 1)
+        return ((t, sp + 2), fits & right, 3, 0), ((t, sp - 1), fits & left, 0, 3)
+
+    for n in range(len(PIECES)):
+        senders.extend(piece_sources(n))
+        for early in (True, False):
+            receivers.extend(there for _, there, _, _ in piece_targets(n, early))
+
     for device, there in senders:
         def signal(device=device):
             pl.semaphore_signal(barrier, inc=1, device_id=device, device_id_type=MESH)
@@ -166,7 +190,7 @@
 
     pl.semaphore_wait(barrier, sum(jnp.asarray(there).astype(jnp.int32) for there in receivers))
 
-    def unit_copies(unit, at, device, extra=0):
+    def unit_copies(unit, at, device):
         src, dst = pl.ds(unit * W, W), pl.ds(pl.multiple_of(at * W, W), W)
         pairs = ((off_h, win_off), (coarse_h, win_coarse), (rates_h, win_rates), (diag_h, win_diag))
         copies = []
@@ -174,21 +198,38 @@
             if device is None:
                 copies.append(pltpu.make_async_copy(a.at[src], b.at[dst], unit_recv.at[at, n]))
             else:
-                copies.append(remote(a.at[src], b.at[dst], unit_send.at[4 if extra else unit, n], unit_recv.at[at, n], device))
+                copies.append(remote(a.at[src], b.at[dst], unit_send.at[unit, n], unit_recv.at[at, n], device))
         return copies
 
     def unit_plan():
         plan = []
         for unit in range(4):
             at = unit - 2 * mine + 1
-            plan.append((unit, at, (tm, sp + 1), (core == 0) & (at >= 0) & (at < 4), 0))
+            plan.append((unit, at, (tm, sp + 1), (core == 0) & (at >= 0) & (at < 4)))
             at = unit + 4 - 2 * mine + 1
-            plan.append((unit, at, None, on_chain & (at >= 0) & (at < 4), 0))
-        next_low = quarter(chip + 1, line) == 0
-        plan.append((3, 0, (tm, sp + 2), on_chain & (chip < n_sp // 2 - 1) & next_low, 1))
-        last_high = quarter(chip - 1, line) == GROUP - 1
-        plan.append((0, 3, (tm, sp - 1), (core == 0) & (chip > 0) & last_high, 1))
+            plan.append((unit, at, None, on_chain & (at >= 0) & (at < 4)))
         return plan
+
+    def piece_copies(n, unit, at, device, row):
+        first, count = PIECES[n][2:]
+        src, dst = pl.ds(unit * W + first, count), pl.ds(at * W + first, count)
+        copies = [
+            remote(off_h.at[src], win_off.at[dst], piece_send.at[row, 0], piece_recv.at[n, 0], device),
+            remote(coarse_h.at[src], win_coarse.at[dst], piece_send.at[row, 1], piece_recv.at[n, 1], device),
+        ]
+        if n == 0:
+            src, dst = pl.ds(unit * W, W), pl.ds(at * W, W)
+            copies.append(remote(rates_h.at[src], win_rates.at[dst], piece_send.at[row, 2], piece_recv.at[n, 2], device))
+        return copies
+
+    def pieces(early, act):
+        for n in range(len(PIECES)):
+            for device, there, unit, at in piece_targets(n, early):
+                def go(n=n, unit=unit, at=at, device=device):
+                    for copy in piece_copies(n, unit, at, device, n if early else n + len(PIECES)):
+                        act(copy)
+
+                pl.when(there)(go)
 
     def cols_copy(which):
         slot, device = ((1, (tm, sp + 1)), (3, (tm, sp - 1)), (0, (tm, sp + 2)))[which]
@@ -206,9 +247,9 @@
     def weights_out():
         for which, there in cols_plan():
             pl.when(there)(cols_copy(which).start)
-        for unit, at, device, there, extra in unit_plan():
-            def go(unit=unit, at=at, device=device, extra=extra):
-                copies = unit_copies(unit, at, device, extra)
+        for unit, at, device, there in unit_plan():
+            def go(unit=unit, at=at, device=device):
+                copies = unit_copies(unit, at, device)
                 for copy in copies[:3]:
                     copy.start()
                 pl.when((at == 1) | (at == 2))(copies[3].start)
@@ -218,19 +259,20 @@
     def weights_sent():
         for which, there in cols_plan():
             pl.when(there)(cols_copy(which).wait_send)
-        for unit, at, device, there, extra in unit_plan():
+        for unit, at, device, there in unit_plan():
             if device is None:
                 continue
 
-            def done(unit=unit, at=at, device=device, extra=extra):
-                copies = unit_copies(unit, at, device, extra)
+            def done(unit=unit, at=at, device=device):
+                copies = unit_copies(unit, at, device)
                 for copy in copies[:3]:
                     copy.wait_send()
                 pl.when((at == 1) | (at == 2))(copies[3].wait_send)
 
             pl.when(there)(done)
 
-    pl.when(plane == chain_plane(0))(weights_out)
+    pieces(True, lambda copy: copy.start())
+    pl.when(plane == first_plane)(weights_out)
 
     def halo_copies(kind, count):
         to_left = remote(
@@ -526,14 +568,18 @@
         to_scalars = pltpu.make_async_copy(cols_land, cols_s, cols_send.at[3])
         to_scalars.start()
         for at in range(4):
-            there = (first_unit + at >= 0) | (chip > 0)
-            there = there & ((first_unit + at < 8) | (chip < n_sp // 2 - 1))
-
-            @pl.when(there)
+            @pl.when((first_unit + at >= 0) & (first_unit + at < 8))
             def _(at=at):
                 copies = unit_copies(0, at, (tm, sp))
                 for copy in copies[:3] if at in (0, 3) else copies:
                     copy.wait_recv()
+
+        for n in range(len(PIECES)):
+            for at, there in ((0, lower), (3, upper)):
+                @pl.when(there)
+                def _(n=n, at=at):
+                    for copy in piece_copies(n, 0, at, (tm, sp), n):
+                        copy.wait_recv()
 
         to_scalars.wait()
 
@@ -641,7 +687,11 @@
 
     def round_of(it, carry):
         fine(it)
-        pl.when((it == 0) & (plane != chain_plane(0)))(weights_out)
+
+        @pl.when((it == 0) & (plane != first_plane))
+        def _():
+            pieces(False, lambda copy: copy.start())
+            weights_out()
 
         @pl.when(on_chain & ((group < 2) == (it == 0)))
         def _():
@@ -669,6 +719,8 @@
     rows_loop(0, rows // 4, write)
 
     weights_sent()
+    for early in (True, False):
+        pieces(early, lambda copy: copy.wait_send())
     for copy, there in start_copies():
         pl.when(there)(copy.wait_send)
     for it in range(ITERS):
@@ -725,7 +777,8 @@
         tiles(ITERS, 2, rows // 4), tiles(2, 2, edge),
         pltpu.VMEM((4, 1, BS), jnp.int32), pltpu.SMEM((4, 1, BS), jnp.int32),
         pltpu.SMEM((rows, K), jnp.int32), pltpu.SMEM((WINDOW, K), jnp.int32),
-        dma((8,)), dma((3, 2)), dma((3, 2)), dma((5, 4)), dma((4, 4)), dma((4,)), dma((4,)),
+        dma((8,)), dma((3, 2)), dma((3, 2)), dma((4, 4)), dma((4, 4)), dma((4,)), dma((4,)),
+        dma((2 * len(PIECES), 3)), dma((len(PIECES), 3)),
         dma((ITERS, 6)), dma((slots, 3)), dma((6,)), dma((slots, 3)), dma((slots, 3)),
         dma((slots, 2, 2)), dma((ITERS, 2, 4)),
     ]
@@ -736,7 +789,7 @@
         out_specs=vmem,
         scratch_shapes=scratch,
         compiler_params=pltpu.CompilerParams(
-            collective_id=0, has_side_effects=True, vmem_limit_bytes=48 << 20
+            collective_id=0, has_side_effects=True, vmem_limit_bytes=60 << 20
         ),
     )(start, guess, columns.reshape(1, rows * K), rates.reshape(rows, BS), mixing, diag, off, fine, coarse)
 

time: 116 us -> 102 us (0.88)
  Pallas kernels: 107 us -> 98.5 us
  local copies, waits for them, and re-layouts: 8.29 us -> 3 us
    pallas_call x1, Pallas kernels: 107 us -> 98.5 us  [shards(): pl.pallas_call(functools.partial(kernel, n_tm, n_sp, rows), out_shape=jax...]
    unnamed x16 -> x2, local copies, waits for them, and re-layouts: 8.19 us -> 2.38 us
where the time goes in v3:
time: 102 us
  Pallas kernels  98.5 us (97%)
  local copies, waits for them, and re-layouts  3 us (3%)
    pallas_call x1, Pallas kernels, shards(): pl.pallas_call(functools.partial(kernel, n_tm, n_sp, rows), out_shape=jax...  98.5 us
    unnamed x2, local copies, waits for them, and re-layouts  2.38 us

profile of v3, /device:TPU:120, one launch (start us, length us, event | category | flops | bytes accessed | tf_op | source)
XLA Modules:
  0.0 101.5 jit_solution(12305972976876282588)
XLA Ops:
  0.0 0.8 copy.11
  0.8 0.6 reshape.6.cols_h
  1.4 98.5 %shard_map.91 = f32[1,3,4,4096]{3,2,1,0:T(4,128)} custom-call(f32[4,4096]{1,0:T(4,128)} %start_h.1, f32[1,4,4096]{2,1,0:T(4,128)} %guess_h.1, s32[1,128]{1,0:T(1,128)} %reshape.6.cols_h, f32[32,128]{1,0:T(8,128)} %bitcast.1, f32[4,4]{1,0:T(4,128)} %mixing_h.1, bf16[32,128,128]{2,1,0:T(8,128)(2,1)} %diag_h.1, bf16[32,4,128,128]{3,2,1,0:T(8,128)(2,1)} %off_h.1, ...), custom_call_target="tpu_custom_call" | custom-call | tf_op jit(solution)/shard_map/pallas_call | solution.py:785
  99.9 1.6 %copy.13 = f32[1,3,4,4096]{3,2,1,0:T(4,128)} copy(f32[1,3,4,4096]{3,2,1,0:T(4,128)} %shard_map.91) | data formatting | bytes 393216

commit v4 on v3

--- a/solution.py
+++ b/solution.py
@@ -21,7 +21,9 @@
 OWN = 16
 WINDOW = OWN + 2 * W
 T_OWN, T_WINDOW, T_EDGE = OWN // 4, WINDOW // 4, W // 4
-PIECES = ((0, 0, 0, 1), (0, 1, 1, 2), (0, GROUP - 1, 3, 1), (1, 0, 4, 2), (GROUP - 1, 0, 6, 2))
+PIECES = ((0, 1), (1, 2), (3, 1), (4, 2), (6, 2))
+FIRST_FROM = ((0, 0), (0, 1), (0, GROUP - 1), (1, 0), (GROUP - 1, 0))
+OTHERS_FROM = ((0, 0), (0, 1), (0, GROUP - 1), (0, 0), (0, GROUP - 1))
 
 
 def dot(lhs, rhs):
@@ -137,23 +139,26 @@
     upper = on_chain & (mine == GROUP - 1) & (chip < n_sp // 2 - 1)
 
     def piece_sources(n):
-        z = jnp.where(plane == first_plane, (plane + PIECES[n][0]) % GROUP, plane)
-        t = z * GROUP + (line + PIECES[n][1]) % GROUP
+        t_first, t_others = (
+            (plane + dz) % GROUP * GROUP + (line + dy) % GROUP for dz, dy in (FIRST_FROM[n], OTHERS_FROM[n])
+        )
+        t = jnp.where(plane == first_plane, t_first, t_others)
         return ((t, sp - 2), lower), ((t, sp + 1), upper)
 
-    def piece_targets(n, early):
-        z = (plane + GROUP - PIECES[n][0]) % GROUP if early else plane
-        y = (line + GROUP - PIECES[n][1]) % GROUP
+    def piece_targets(n, when):
+        dz, dy = OTHERS_FROM[n] if when else FIRST_FROM[n]
+        z, y = (plane + GROUP - dz) % GROUP, (line + GROUP - dy) % GROUP
         t = z * GROUP + y
-        fits = (z == first_plane) if early else (z != first_plane)
+        hurried = z == 0
+        fits = z == first_plane if when == 0 else (z != first_plane) & ~hurried if when == 1 else hurried
         right = on_chain & (chip < n_sp // 2 - 1) & (quarter(chip + 1, y) == 0)
         left = ~on_chain & (chip > 0) & (quarter(chip - 1, y) == GROUP - 1)
         return ((t, sp + 2), fits & right, 3, 0), ((t, sp - 1), fits & left, 0, 3)
 
     for n in range(len(PIECES)):
         senders.extend(piece_sources(n))
-        for early in (True, False):
-            receivers.extend(there for _, there, _, _ in piece_targets(n, early))
+        for when in range(3):
+            receivers.extend(there for _, there, _, _ in piece_targets(n, when))
 
     for device, there in senders:
         def signal(device=device):
@@ -163,20 +168,6 @@
 
     for load in small:
         load.wait()
-
-    def local_place(b, carry):
-        for k in range(K):
-            place_of[b, k] = jnp.clip(cols[0, b * K + k] - (sp * rows - W), 0, rows + 2 * W - 1)
-        return carry
-
-    lax.fori_loop(0, rows, local_place, 0)
-    near[...] = jnp.zeros_like(near)
-    near_q[...] = jnp.zeros_like(near_q)
-    imp_b[...] = jnp.zeros_like(imp_b)
-    exp_b[...] = jnp.zeros_like(exp_b)
-    for t in range(SPECIES):
-        column = jnp.broadcast_to(mixing[:, t : t + 1], (SPECIES, BS))
-        mix_v[t] = jnp.concatenate([column, column], axis=0)
 
     def cells(b):
         return pl.ds(pl.multiple_of(b * BS, BS), BS)
@@ -211,7 +202,7 @@
         return plan
 
     def piece_copies(n, unit, at, device, row):
-        first, count = PIECES[n][2:]
+        first, count = PIECES[n]
         src, dst = pl.ds(unit * W + first, count), pl.ds(at * W + first, count)
         copies = [
             remote(off_h.at[src], win_off.at[dst], piece_send.at[row, 0], piece_recv.at[n, 0], device),
@@ -222,11 +213,11 @@
             copies.append(remote(rates_h.at[src], win_rates.at[dst], piece_send.at[row, 2], piece_recv.at[n, 2], device))
         return copies
 
-    def pieces(early, act):
+    def pieces(when, act):
         for n in range(len(PIECES)):
-            for device, there, unit, at in piece_targets(n, early):
+            for device, there, unit, at in piece_targets(n, when):
                 def go(n=n, unit=unit, at=at, device=device):
-                    for copy in piece_copies(n, unit, at, device, n if early else n + len(PIECES)):
+                    for copy in piece_copies(n, unit, at, device, n + when * len(PIECES)):
                         act(copy)
 
                 pl.when(there)(go)
@@ -271,8 +262,6 @@
 
             pl.when(there)(done)
 
-    pieces(True, lambda copy: copy.start())
-    pl.when(plane == first_plane)(weights_out)
 
     def halo_copies(kind, count):
         to_left = remote(
@@ -389,10 +378,18 @@
             (piece(t_rows + T_OWN, T_OWN, rest, 5, 2, to[1]), True),
         )
 
+    def terms_sent(it):
+        for copy, there in terms_copies(it):
+            if there is True:
+                copy.wait_send()
+            else:
+                pl.when(there)(copy.wait_send)
+
     def fine(it):
         @pl.when(it == 0)
         def _():
             halo_send(NODES, [lambda b: nodes[b, 0:4], lambda b: nodes[b, 4:8]])
+            first_things()
             for load in large:
                 load.wait()
             lax.fori_loop(0, rows // 4, transposed, 0)
@@ -455,6 +452,7 @@
             near[W + b, 0:4] = first_v[b]
 
         rows_loop(0, rows, put_first)
+        early_units(it, 0)
         halo_wait(FIRST, 1)
         halo_place(FIRST, near, 1)
 
@@ -492,6 +490,7 @@
                 exp_b[b] += -0.5 * exp
 
         inner(second_terms)
+        early_units(it, 1)
         halo_wait(SECOND, 1)
         halo_place(SECOND, near, 1)
         outer(second_terms)
@@ -553,59 +552,104 @@
                 chain_recv.at[0, part], chain_device(i, chain_plane(0))), (tm == 0) & ok))
         return copies
 
-    @pl.when(tm == 0)
-    def _():
-        for j in range(rows // 4):
-            start_b[j] = tile([nodes[4 * j + g, 0:4] for g in range(4)])
-        for copy, there in start_copies():
-            pl.when(there)(copy.start)
-
-    def window_weights():
+    def first_things():
+        pieces(0, lambda copy: copy.start())
+        pl.when(plane == first_plane)(weights_out)
+        def local_place(b, carry):
+            for k in range(K):
+                place_of[b, k] = jnp.clip(cols[k, b] - (sp * rows - W), 0, rows + 2 * W - 1)
+            return carry
+
+        lax.fori_loop(0, rows, local_place, 0)
+        near[...] = jnp.zeros_like(near)
+        near_q[...] = jnp.zeros_like(near_q)
+        imp_b[...] = jnp.zeros_like(imp_b)
+        exp_b[...] = jnp.zeros_like(exp_b)
+        for t in range(SPECIES):
+            column = jnp.broadcast_to(mixing[:, t : t + 1], (SPECIES, BS))
+            mix_v[t] = jnp.concatenate([column, column], axis=0)
+
+        @pl.when(tm == 0)
+        def _():
+            for j in range(rows // 4):
+                start_b[j] = tile([nodes[4 * j + g, 0:4] for g in range(4)])
+            for copy, there in start_copies():
+                pl.when(there)(copy.start)
+
+    def composed(n, carry):
+        for r in range(4):
+            w = 4 * n + r
+            inverse = win_coarse[w].T
+            comp_w[w, BS : 2 * BS] = inverse
+            inverse_w[2 * n + r // 2, :, BS * (r % 2) : BS * (r % 2 + 1)] = inverse
+            raw = [win_diag[w]] + [win_off[w, k] for k in range(K)]
+            got = (dot(jnp.concatenate([block.T for block in raw], axis=0), inverse) * STEP).astype(jnp.bfloat16)
+            comp_w[w, :BS] = got[:BS]
+            comp_w[w, 2 * BS :] = got[BS:]
+        return carry
+
+    def window_unit(at, foreign=True):
+        unit = 2 * mine - 1 + at
+
+        @pl.when((unit >= 0) & (unit < 8))
+        def _():
+            copies = unit_copies(0, at, (tm, sp))
+            for copy in copies[:3] if at in (0, 3) else copies:
+                copy.wait_recv()
+
+        if at in (0, 3) and foreign:
+            there = lower if at == 0 else upper
+            for n in range(len(PIECES)):
+                @pl.when(there)
+                def _(n=n):
+                    for copy in piece_copies(n, 0, at, (tm, sp), n):
+                        copy.wait_recv()
+
+        lax.fori_loop(W // 4 * at, W // 4 * (at + 1), composed, 0)
+
+    def window_places():
         first_unit = 2 * mine - 1
         arrive(cols_land.at[1], cols_recv.at[1])
-        arrive(cols_land.at[0], cols_recv.at[0], (mine == 0) & (chip > 0))
-        arrive(cols_land.at[3], cols_recv.at[3], (mine == GROUP - 1) & (chip < n_sp // 2 - 1))
+        arrive(cols_land.at[0], cols_recv.at[0], lower)
+        arrive(cols_land.at[3], cols_recv.at[3], upper)
         to_scalars = pltpu.make_async_copy(cols_land, cols_s, cols_send.at[3])
         to_scalars.start()
-        for at in range(4):
-            @pl.when((first_unit + at >= 0) & (first_unit + at < 8))
-            def _(at=at):
-                copies = unit_copies(0, at, (tm, sp))
-                for copy in copies[:3] if at in (0, 3) else copies:
-                    copy.wait_recv()
-
-        for n in range(len(PIECES)):
-            for at, there in ((0, lower), (3, upper)):
-                @pl.when(there)
-                def _(n=n, at=at):
-                    for copy in piece_copies(n, 0, at, (tm, sp), n):
-                        copy.wait_recv()
-
         to_scalars.wait()
 
         def places(w, carry):
             unit = first_unit + w // W
             slot, row = (unit + 4) // 4, (unit + 4) % 4 * W + w % W
             for k in range(K):
-                column = jnp.where(slot == 2, cols[0, row * K + k], cols_s[slot, 0, row * K + k])
+                column = jnp.where(slot == 2, cols[k, row], cols_s[slot, k, row])
                 place_w[w, k] = jnp.clip(column - (chunk * OWN - 2 * W), 0, OWN + 4 * W - 1)
             return carry
 
         lax.fori_loop(0, WINDOW, places, 0)
 
-        def composed(n, carry):
-            for r in range(4):
-                w = 4 * n + r
-                inverse = win_coarse[w].T
-                comp_w[w, BS : 2 * BS] = inverse
-                inverse_w[2 * n + r // 2, :, BS * (r % 2) : BS * (r % 2 + 1)] = inverse
-                raw = [win_diag[w]] + [win_off[w, k] for k in range(K)]
-                got = (dot(jnp.concatenate([block.T for block in raw], axis=0), inverse) * STEP).astype(jnp.bfloat16)
-                comp_w[w, :BS] = got[:BS]
-                comp_w[w, 2 * BS :] = got[BS:]
-            return carry
-
-        lax.fori_loop(0, WINDOW // 4, composed, 0)
+    hurry = on_chain & (plane == first_plane)
+
+    def early_units(it, step):
+        @pl.when((it == 0) & hurry)
+        def _():
+            if step == 0:
+                window_places()
+                window_unit(1)
+            else:
+                window_unit(2)
+                pl.when(mine != GROUP - 1)(functools.partial(window_unit, 3, False))
+                pl.when(mine == GROUP - 1)(functools.partial(window_unit, 0, False))
+
+    def window_weights():
+        @pl.when(~hurry)
+        def _():
+            window_places()
+            for at in range(4):
+                window_unit(at)
+
+        @pl.when(hurry)
+        def _():
+            pl.when(mine == GROUP - 1)(functools.partial(window_unit, 3))
+            pl.when(mine != GROUP - 1)(functools.partial(window_unit, 0))
 
     def chain_step(g, carry):
         it, j = g // GROUP, g % GROUP
@@ -688,19 +732,43 @@
     def round_of(it, carry):
         fine(it)
 
-        @pl.when((it == 0) & (plane != first_plane))
-        def _():
-            pieces(False, lambda copy: copy.start())
-            weights_out()
+        @pl.when(it == 0)
+        def _():
+            terms_sent(0)
+            pieces(1, lambda copy: copy.start())
+            pieces(2, lambda copy: copy.start())
+            pl.when(plane != first_plane)(weights_out)
+
+        composes = jnp.where((plane == 0) & (line == 0), 1, 0)
+        pl.when(on_chain & (it == composes))(window_weights)
 
         @pl.when(on_chain & ((group < 2) == (it == 0)))
         def _():
-            window_weights()
             lax.fori_loop(0, ITERS * GROUP, chain_step, 0)
 
         return carry
 
     lax.fori_loop(0, ITERS, round_of, 0)
+
+    weights_sent()
+    for when in range(3):
+        pieces(when, lambda copy: copy.wait_send())
+    for copy, there in start_copies():
+        pl.when(there)(copy.wait_send)
+    terms_sent(1)
+
+    @pl.when(on_chain)
+    def _():
+        def sent(g, carry):
+            it, j = g // GROUP, g % GROUP
+            for copy, there in chain_copies(it, j) + value_copies(it, j):
+                if there is True:
+                    copy.wait_send()
+                else:
+                    pl.when(there)(copy.wait_send)
+            return carry
+
+        lax.fori_loop(0, ITERS * GROUP, sent, 0)
 
     pl.when(tm > 0)(lambda: values_wait(1, 0, False))
     values_wait(1, 1, False)
@@ -718,31 +786,6 @@
 
     rows_loop(0, rows // 4, write)
 
-    weights_sent()
-    for early in (True, False):
-        pieces(early, lambda copy: copy.wait_send())
-    for copy, there in start_copies():
-        pl.when(there)(copy.wait_send)
-    for it in range(ITERS):
-        for copy, there in terms_copies(it):
-            if there is True:
-                copy.wait_send()
-            else:
-                pl.when(there)(copy.wait_send)
-
-    @pl.when(on_chain)
-    def _():
-        def sent(g, carry):
-            it, j = g // GROUP, g % GROUP
-            for copy, there in chain_copies(it, j) + value_copies(it, j):
-                if there is True:
-                    copy.wait_send()
-                else:
-                    pl.when(there)(copy.wait_send)
-            return carry
-
-        lax.fori_loop(0, ITERS * GROUP, sent, 0)
-
 
 def shards(n_tm, n_sp, start, guess, diag, off, columns, rates, mixing, fine, coarse):
     rows = diag.shape[0]
@@ -762,7 +805,7 @@
     pairs = pltpu.VMEM((rows // 2, BS, 2 * BS), bf16)
     scratch = [
         pltpu.VMEM((SPECIES, rows * BS), f32), pltpu.VMEM((1, SPECIES, rows * BS), f32),
-        pltpu.SMEM((1, rows * K), jnp.int32), pltpu.VMEM((rows, BS), f32), pltpu.VMEM((SPECIES, SPECIES), f32),
+        pltpu.SMEM((K, rows), jnp.int32), pltpu.VMEM((rows, BS), f32), pltpu.VMEM((SPECIES, SPECIES), f32),
         blocks(rows), blocks(rows, K), blocks(rows),
         pltpu.VMEM((rows, K * BS, BS), bf16), pairs, pairs,
         blocks(WINDOW), blocks(WINDOW, K), blocks(WINDOW), pltpu.VMEM((WINDOW, BS), f32),
@@ -775,10 +818,10 @@
         tiles(ITERS, rows // 2), tiles(slots, T_WINDOW), tiles(slots, T_OWN),
         tiles(rows // 4), tiles(slots, 3, T_OWN), tiles(slots, T_OWN),
         tiles(ITERS, 2, rows // 4), tiles(2, 2, edge),
-        pltpu.VMEM((4, 1, BS), jnp.int32), pltpu.SMEM((4, 1, BS), jnp.int32),
+        pltpu.VMEM((4, K, rows), jnp.int32), pltpu.SMEM((4, K, rows), jnp.int32),
         pltpu.SMEM((rows, K), jnp.int32), pltpu.SMEM((WINDOW, K), jnp.int32),
         dma((8,)), dma((3, 2)), dma((3, 2)), dma((4, 4)), dma((4, 4)), dma((4,)), dma((4,)),
-        dma((2 * len(PIECES), 3)), dma((len(PIECES), 3)),
+        dma((3 * len(PIECES), 3)), dma((len(PIECES), 3)),
         dma((ITERS, 6)), dma((slots, 3)), dma((6,)), dma((slots, 3)), dma((slots, 3)),
         dma((slots, 2, 2)), dma((ITERS, 2, 4)),
     ]
@@ -791,7 +834,7 @@
         compiler_params=pltpu.CompilerParams(
             collective_id=0, has_side_effects=True, vmem_limit_bytes=60 << 20
         ),
-    )(start, guess, columns.reshape(1, rows * K), rates.reshape(rows, BS), mixing, diag, off, fine, coarse)
+    )(start, guess, columns.T, rates.reshape(rows, BS), mixing, diag, off, fine, coarse)
 
 
 def solution(mesh):

time: 102 us -> 97.2 us (0.953)
  Pallas kernels: 98.5 us -> 95.5 us
  local copies, waits for them, and re-layouts: 3 us -> 1.62 us
    pallas_call x1, Pallas kernels: 98.5 us -> 95.5 us  [shards(): pl.pallas_call(functools.partial(kernel, n_tm, n_sp, rows), out_shape=jax...]
    unnamed x2 -> x1, local copies, waits for them, and re-layouts: 2.38 us -> 1.62 us
where the time goes in v4:
time: 97.2 us; the launch traced here: 97.1 us
  Pallas kernels  95.5 us (98%)
  local copies, waits for them, and re-layouts  1.62 us (2%)
    pallas_call x1, Pallas kernels, shards(): pl.pallas_call(functools.partial(kernel, n_tm, n_sp, rows), out_shape=jax...  95.5 us

profile of v4, /device:TPU:120, one launch (start us, length us, event | category | flops | bytes accessed | tf_op | source)
XLA Modules:
  0.0 97.1 jit_solution(11345515611054242990)
XLA Ops:
  0.0 95.5 %shard_map.91 = f32[1,3,4,4096]{3,2,1,0:T(4,128)} custom-call(f32[4,4096]{1,0:T(4,128)} %start_h.1, f32[1,4,4096]{2,1,0:T(4,128)} %guess_h.1, s32[4,32]{1,0:T(4,128)} %bitcast.3, f32[32,128]{1,0:T(8,128)} %bitcast.2, f32[4,4]{1,0:T(4,128)} %mixing_h.1, bf16[32,128,128]{2,1,0:T(8,128)(2,1)} %diag_h.1, bf16[32,4,128,128]{3,2,1,0:T(8,128)(2,1)} %off_h.1, ...), custom_call_target="tpu_custom_call" | custom-call | tf_op jit(solution)/shard_map/pallas_call | solution.py:828
  95.5 1.6 %copy.11 = f32[1,3,4,4096]{3,2,1,0:T(4,128)} copy(f32[1,3,4,4096]{3,2,1,0:T(4,128)} %shard_map.91) | data formatting | bytes 393216

commit v5 on v4

--- a/solution.py
+++ b/solution.py
@@ -18,6 +18,7 @@
 NODES, FIRST, SECOND = range(3)
 LEFT, RIGHT = 0, 1
 GROUP = 4
+STRETCH = 8
 OWN = 16
 WINDOW = OWN + 2 * W
 T_OWN, T_WINDOW, T_EDGE = OWN // 4, WINDOW // 4, W // 4
@@ -48,7 +49,7 @@
     diag_v, off_v, fine_v, raw_w, diag_w, fine_w, win_diag, win_off, win_coarse, win_rates, comp_w, inverse_w,
     near, near_q, mix_v, nodes, imp_b, exp_b, mid_b, first_v, second_r,
     sum_c, sum_t, state, solved, partial, fresh, right_v,
-    send_b, land, terms_b, terms_land, rest_land, start_b, chain_land, end_b, value_land, value_halo,
+    send_b, land, terms_b, terms_land, start_b, chain_land, end_b, value_land, value_halo,
     cols_land, cols_s, place_of, place_w,
     load_sem, send_sem, recv_sem, unit_send, unit_recv, cols_send, cols_recv, piece_send, piece_recv,
     terms_send, terms_recv, start_send, chain_send, chain_recv, value_send, value_recv,
@@ -67,12 +68,12 @@
         x, j = i // GROUP, i % GROUP
         return z * GROUP + quarter(x, j), 2 * x + 1
 
-    def chain_plane(group):
-        return (group + 2) % GROUP
+    def chain_plane(it, p):
+        return jnp.where(p < STRETCH, 2, 0) + it
 
     mine = quarter(chip, line)
     chunk = GROUP * chip + mine
-    group = (plane + 2) % GROUP
+    round_here, stretch = plane % 2, jnp.where(plane < 2, 1, 0)
     on_chain = core == 1
     even = chunk % 2 == 0
     chunk_left, chunk_right = chunk > 0, chunk < chunks - 1
@@ -109,10 +110,13 @@
     cols_land[...] = jnp.zeros_like(cols_land)
 
     barrier = pltpu.get_barrier_semaphore()
-    my_plane = chain_plane(plane)
-    later, before = group < GROUP - 1, group > 0
-    after, earlier = (plane + 1) % GROUP, (plane + GROUP - 1) % GROUP
+    later = stretch == 0
     senders, receivers = [], []
+    own_next = ((stretch + 1) * STRETCH == tm) & (owner == sp)
+
+    def is_me(device):
+        return (device[0] == tm) & (device[1] == sp)
+
 
     def both(device, there):
         senders.append((device, there))
@@ -121,20 +125,22 @@
     both((tm, sp - 1), has_left)
     both((tm, sp + 1), has_right)
     for i, there in ((low - 1, has_left), (low, True), (high, True), (high + 1, has_right)):
-        both(chain_device(i, my_plane), there)
-        senders.append((chain_device(i, chain_plane(plane + GROUP - 1)), there & (line == 0) & (plane > 0)))
-    for y in range(GROUP):
-        both((group * GROUP + y, owner), on_chain)
-        both((group * GROUP + y, beside), on_chain & has_beside)
-    receivers.append(on_chain & later)
+        for it in range(ITERS):
+            both(chain_device(i, chain_plane(it, tm)), there)
+            device = chain_device(i, chain_plane(it, 0))
+            senders.append((device, there & (tm == STRETCH) & ~is_me(device)))
+    for j in range(STRETCH):
+        both((stretch * STRETCH + j, owner), on_chain)
+        both((stretch * STRETCH + j, beside), on_chain & has_beside)
+    receivers.append(on_chain & later & ~own_next)
     receivers.append(on_chain & later & has_beside)
     both(chain_device(chunk - 1, plane), on_chain & chunk_left)
     both(chain_device(chunk + 1, plane), on_chain & chunk_right)
     for i, there in ((chunk, True), (chunk - 1, chunk_left), (chunk + 1, chunk_right)):
-        senders.append((chain_device(i, earlier), on_chain & before & there))
+        senders.append((chain_device(i, plane + 2), on_chain & ~later & there))
         receivers.append(on_chain & later & there)
 
-    first_plane = chain_plane(0)
+    first_plane = 2
     lower = on_chain & (mine == 0) & (chip > 0)
     upper = on_chain & (mine == GROUP - 1) & (chip < n_sp // 2 - 1)
 
@@ -358,28 +364,38 @@
 
         return pair
 
-    def terms_copies(it):
-        slot = it * GROUP + line
-        main, rest = terms_land.at[slot], rest_land.at[slot]
-        to = [chain_device(i, my_plane) for i in (low, high, low - 1, high + 1)]
-
-        def piece(first, count, dst, n, sem, device):
+    def terms_copies(it, late):
+        slot = tm % STRETCH
+        main = terms_land.at[slot]
+        to = [chain_device(i, chain_plane(it, tm)) for i in (low, high, low - 1, high + 1)]
+
+        def piece(first, count, at, n, sem, device):
             return remote(
-                terms_b.at[it, pl.ds(first, count)], dst, terms_send.at[it, n], terms_recv.at[slot, sem], device
+                terms_b.at[it, pl.ds(first, count)], main.at[pl.ds(at, count)], terms_send.at[it, n],
+                terms_recv.at[slot, sem], device,
             )
 
-        t_rows = rows // 4
-        return (
-            (piece(0, 6, main.at[pl.ds(2, 6)], 0, 0, to[0]), True),
-            (piece(2, 6, main.at[pl.ds(0, 6)], 1, 0, to[1]), True),
-            (piece(0, 2, main.at[pl.ds(6, 2)], 2, 1, to[2]), has_left),
-            (piece(6, 2, main.at[pl.ds(0, 2)], 3, 1, to[3]), has_right),
-            (piece(t_rows, T_OWN, rest, 4, 2, to[0]), True),
-            (piece(t_rows + T_OWN, T_OWN, rest, 5, 2, to[1]), True),
-        )
+        if late:
+            return (
+                (piece(0, 2, 2, 0, 0, to[0]), True),
+                (piece(6, 2, 4, 1, 0, to[1]), True),
+                (piece(0, 2, 6, 2, 1, to[2]), has_left),
+                (piece(6, 2, 0, 3, 1, to[3]), has_right),
+            )
+        return (piece(2, 4, 4, 4, 2, to[0]), True), (piece(2, 4, 0, 5, 2, to[1]), True)
+
+    def terms_out(it, late):
+        for j in (0, 1, 6, 7) if late else range(2, 6):
+            terms_b[it, j, 0] = tile([sum_c[4 * j + g] for g in range(4)])
+            terms_b[it, j, 1] = tile([sum_t[4 * j + g] for g in range(4)])
+        for copy, there in terms_copies(it, late):
+            if there is True:
+                copy.start()
+            else:
+                pl.when(there)(copy.start)
 
     def terms_sent(it):
-        for copy, there in terms_copies(it):
+        for copy, there in terms_copies(it, True) + terms_copies(it, False):
             if there is True:
                 copy.wait_send()
             else:
@@ -393,6 +409,8 @@
             for load in large:
                 load.wait()
             lax.fori_loop(0, rows // 4, transposed, 0)
+            for b in range(rows):
+                near[W + b] = nodes[b]
             halo_wait(NODES, 2)
             halo_place(NODES, near, 2)
 
@@ -403,27 +421,26 @@
                 values_wait(0, 0, True)
                 for j in range(rows // 4):
                     spread(value_land[0, 0, j], nodes, 4 * j, 0)
+                    spread(value_land[0, 0, j], near, W + 4 * j, 0)
                 for j in range(edge):
                     spread(value_halo[0, LEFT, j], near, 4 * j, 0)
                     spread(value_halo[0, RIGHT, j], near, W + rows + 4 * j, 0)
 
             @pl.when(tm == 0)
             def _():
+                for b in range(rows):
+                    near[W + b, 0:4] = nodes[b, 0:4]
                 for j in range(edge):
                     spread(land[NODES, LEFT, j], near, 4 * j, 0)
                     spread(land[NODES, RIGHT, j], near, W + rows + 4 * j, 0)
 
             values_wait(0, 1, True)
             for j in range(rows // 4):
-                spread(value_land[0, 1, j], nodes, 4 * j, 4)
+                spread(value_land[0, 1, j], near, W + 4 * j, 4)
             for j in range(edge):
                 spread(value_halo[1, LEFT, j], near, 4 * j, 4)
                 spread(value_halo[1, RIGHT, j], near, W + rows + 4 * j, 4)
 
-        def place(b):
-            near[W + b] = nodes[b]
-
-        rows_loop(0, rows, place)
         own_part = jnp.where(it == 0, 0.0, 0.5)
         end_part = jnp.where(it == 0, 1.0, 0.5)
 
@@ -446,6 +463,7 @@
 
         outer(node_terms, solve(first_v))
         halo_send(FIRST, [lambda b: first_v[b]])
+        pl.when((it == 0) & (tm == 0))(start_out)
         inner(node_terms, solve(first_v))
 
         def put_first(b):
@@ -470,6 +488,12 @@
 
         outer(first_terms, solve(fresh))
         halo_send(SECOND, [lambda b: fresh[b]])
+
+        @pl.when((it == 0) & (tm == 0))
+        def _():
+            for copy, there in start_copies(1):
+                pl.when(there)(copy.start)
+
         inner(first_terms, solve(fresh))
 
         def put_second(b):
@@ -490,18 +514,12 @@
                 exp_b[b] += -0.5 * exp
 
         inner(second_terms)
+        terms_out(it, False)
         early_units(it, 1)
         halo_wait(SECOND, 1)
         halo_place(SECOND, near, 1)
         outer(second_terms)
-        for j in range(rows // 4):
-            terms_b[it, j] = tile([sum_c[4 * j + g] for g in range(4)])
-            terms_b[it, rows // 4 + j] = tile([sum_t[4 * j + g] for g in range(4)])
-        for copy, there in terms_copies(it):
-            if there is True:
-                copy.start()
-            else:
-                pl.when(there)(copy.start)
+        terms_out(it, True)
 
     def values_wait(it, which, halos):
         for n in range(2):
@@ -510,46 +528,62 @@
             arrive(value_halo.at[which, LEFT], value_recv.at[it, which, 2], has_left)
             arrive(value_halo.at[which, RIGHT], value_recv.at[it, which, 3], has_right)
 
-    def value_copies(it, j):
-        g = it * GROUP + j
-        p = group * GROUP + j
+    def value_copies(j):
+        it, p = round_here, stretch * STRETCH + j
         half = chunk % 2
         copies = []
         for which in (1, 0):
             t = p + 1 - which
-            there = (p < n_tm - 1) if which == 0 else True
+            there = (p < n_tm - 1) & ~((p == STRETCH * (stretch + 1) - 1) & own_next) if which == 0 else True
             copies.append((remote(
-                end_b.at[g], value_land.at[it, which, pl.ds(pl.multiple_of(half * T_OWN, T_OWN), T_OWN)],
-                value_send.at[g, which, 0], value_recv.at[it, which, half], (t, owner)), there))
+                end_b.at[j], value_land.at[it, which, pl.ds(pl.multiple_of(half * T_OWN, T_OWN), T_OWN)],
+                value_send.at[j, which, 0], value_recv.at[it, which, half], (t, owner)), there))
             copies.append((remote(
-                end_b.at[g, pl.ds(pl.multiple_of(half * (T_OWN - T_EDGE), T_EDGE), T_EDGE)], value_halo.at[which, 1 - half],
-                value_send.at[g, which, 1], value_recv.at[it, which, 3 - half], (t, beside)),
-                there & has_beside & (it == 0)))
+                end_b.at[j, pl.ds(pl.multiple_of(half * (T_OWN - T_EDGE), T_EDGE), T_EDGE)], value_halo.at[which, 1 - half],
+                value_send.at[j, which, 1], value_recv.at[it, which, 3 - half], (t, beside)),
+                (t < n_tm) & has_beside & (it == 0)))
         return copies
 
-    def chain_copies(it, j):
-        g = it * GROUP + j
-        inside = j < GROUP - 1
-        target = jnp.where(inside, g + 1, it * GROUP)
-        z = jnp.where(inside, plane, after)
+    def value_here(j):
+        half = chunk % 2
+        return pltpu.make_async_copy(
+            end_b.at[j], value_land.at[round_here, 0, pl.ds(pl.multiple_of(half * T_OWN, T_OWN), T_OWN)],
+            value_recv.at[round_here, 0, half],
+        )
+
+    def chain_copies(j, half):
+        inside = j < STRETCH - 1
+        target = jnp.where(inside, j + 1, 0)
+        z = jnp.where(inside, plane, plane - 2)
         there = inside | later
+        at = pl.ds(half * T_EDGE, T_EDGE)
         copies = []
-        for n, (i, ok) in enumerate(((chunk - 1, chunk_left), (chunk, ~inside), (chunk + 1, chunk_right))):
-            part = 2 - n
+        for n, (i, ok) in enumerate(((chunk - 1, chunk_left), (chunk + 1, chunk_right))):
+            part = 2 - 2 * n
             copies.append((remote(
-                end_b.at[g], chain_land.at[target, part], chain_send.at[g, n], chain_recv.at[target, part],
-                chain_device(i, z)), there & ok))
+                end_b.at[j, at], chain_land.at[target, part, at], chain_send.at[j, 2 * n, half],
+                chain_recv.at[target, part, half], chain_device(i, z)), there & ok))
+        if half == 1:
+            copies.append((remote(
+                end_b.at[j], chain_land.at[target, 1], chain_send.at[j, 1, 0], chain_recv.at[target, 1, 0],
+                chain_device(chunk, z)), there & ~inside))
         return copies
 
-    def start_copies():
+    def start_copies(it):
         copies = []
-        for n, (i, part, half, ok) in enumerate((
+        for n, (i, part, own, ok) in enumerate((
             (low, 1, 0, True), (low, 2, 1, True), (low - 1, 2, 0, has_left),
             (high, 1, 1, True), (high, 0, 0, True), (high + 1, 0, 1, has_right),
         )):
-            copies.append((remote(
-                start_b.at[pl.ds(half * T_OWN, T_OWN)], chain_land.at[0, part], start_send.at[n],
-                chain_recv.at[0, part], chain_device(i, chain_plane(0))), (tm == 0) & ok))
+            device = chain_device(i, chain_plane(it, 0))
+            for half in range(2):
+                count = T_OWN if part == 1 else T_EDGE
+                if part == 1 and half == 1:
+                    continue
+                copies.append((remote(
+                    start_b.at[pl.ds(own * T_OWN + half * T_EDGE, count)],
+                    chain_land.at[0, part, pl.ds(half * T_EDGE, count)], start_send.at[it, n, half],
+                    chain_recv.at[0, part, half], device), (tm == 0) & ok))
         return copies
 
     def first_things():
@@ -569,12 +603,11 @@
             column = jnp.broadcast_to(mixing[:, t : t + 1], (SPECIES, BS))
             mix_v[t] = jnp.concatenate([column, column], axis=0)
 
-        @pl.when(tm == 0)
-        def _():
-            for j in range(rows // 4):
-                start_b[j] = tile([nodes[4 * j + g, 0:4] for g in range(4)])
-            for copy, there in start_copies():
-                pl.when(there)(copy.start)
+    def start_out():
+        for j in range(rows // 4):
+            start_b[j] = tile([nodes[4 * j + g, 0:4] for g in range(4)])
+        for copy, there in start_copies(0):
+            pl.when(there)(copy.start)
 
     def composed(n, carry):
         for r in range(4):
@@ -652,32 +685,27 @@
             pl.when(mine != GROUP - 1)(functools.partial(window_unit, 0))
 
     def chain_step(g, carry):
-        it, j = g // GROUP, g % GROUP
-        from_start = (j == 0) & (group == 0)
-        slot = jnp.where(from_start, 0, g)
-
-        fresh_start = ~(from_start & (it == 1))
-        main_at = jnp.where(even, 2, 0)
         halo_at = jnp.where(even, 0, 6)
-
-        @pl.when(j == 0)
-        def _():
-            arrive(chain_land.at[g, 1], chain_recv.at[g, 1], fresh_start)
+        early_at, late_at = jnp.where(even, 4, 0), jnp.where(even, 2, 4)
+
+        @pl.when(g == 0)
+        def _():
+            arrive(chain_land.at[g, 1], chain_recv.at[g, 1, 0])
             for n in range(T_OWN):
-                spread(chain_land[slot, 1, n], near, 2 * W + 4 * n, 0)
-
-        arrive(terms_land.at[g, pl.ds(main_at, 6)], terms_recv.at[g, 0])
+                spread(chain_land[g, 1, n], near, 2 * W + 4 * n, 0)
+
+        arrive(terms_land.at[g, pl.ds(early_at, 4)], terms_recv.at[g, 2])
+        arrive(terms_land.at[g, pl.ds(late_at, 2)], terms_recv.at[g, 0])
         arrive(terms_land.at[g, pl.ds(halo_at, 2)], terms_recv.at[g, 1], has_beside)
-        arrive(rest_land.at[g], terms_recv.at[g, 2])
 
         def prepare(n):
-            constant = terms_land[g, n].astype(jnp.float32)
+            constant = terms_land[g, n, 0].astype(jnp.float32)
             for r in range(4):
                 w = 4 * n + r
                 own = near[W + w, 0:4]
                 change = STEP * react(own, win_rates[pl.ds(w, 1)])
                 right_v[w, 0:4] = own + change + constant[4 * r : 4 * r + 4]
-                state[w] = own + 0.5 * change
+                state[w] = 2.0 * own + change
             for i in (2 * n, 2 * n + 1):
                 got = paired(right_v[2 * i], right_v[2 * i + 1], inverse_w[i])
                 solved[2 * i], solved[2 * i + 1] = got[0][:4], got[1][:4]
@@ -685,44 +713,49 @@
         rows_loop(T_EDGE, T_WINDOW - T_EDGE, prepare)
 
         def with_rest(n):
-            constant = rest_land[g, n].astype(jnp.float32)
+            constant = terms_land[g, T_EDGE + n, 1].astype(jnp.float32)
             for r in range(4):
-                state[W + 4 * n + r] += constant[4 * r : 4 * r + 4]
+                state[W + 4 * n + r] += 2.0 * constant[4 * r : 4 * r + 4]
 
         rows_loop(0, T_OWN, with_rest)
-
-        @pl.when(fresh_start)
-        def _():
-            arrive(chain_land.at[g, 0], chain_recv.at[g, 0], chunk_left)
-            arrive(chain_land.at[g, 2], chain_recv.at[g, 2], chunk_right)
-
-        for n in range(T_OWN):
-            spread(chain_land[slot, 0, n], near, 4 * n, 0)
-            spread(chain_land[slot, 2, n], near, 2 * W + OWN + 4 * n, 0)
-
-        rows_loop(0, T_EDGE, prepare)
-        rows_loop(T_WINDOW - T_EDGE, T_WINDOW, prepare)
 
         def middle(w):
             spread_s = dot(gather(near, place_w, w), comp_w[w, 2 * BS :])[:4]
             near_q[W + w, 0:4] = solved[w] + spread_s
             partial[w] = 0.5 * spread_s
 
-        rows_loop(0, WINDOW, middle)
+        first, last = pl.ds(0, T_EDGE), pl.ds(T_EDGE, T_EDGE)
+        arrive(chain_land.at[g, 2, first], chain_recv.at[g, 2, 0], chunk_right)
+        for n in range(T_EDGE):
+            spread(chain_land[g, 2, n], near, 2 * W + OWN + 4 * n, 0)
+        rows_loop(T_WINDOW - T_EDGE, T_WINDOW, prepare)
+        rows_loop(2 * W, 2 * W + W, middle)
+        arrive(chain_land.at[g, 0, first], chain_recv.at[g, 0, 0], chunk_left)
+        arrive(chain_land.at[g, 0, last], chain_recv.at[g, 0, 1], chunk_left)
+        arrive(chain_land.at[g, 2, last], chain_recv.at[g, 2, 1], chunk_right)
+        for n in range(T_OWN):
+            spread(chain_land[g, 0, n], near, 4 * n, 0)
+        for n in range(T_EDGE, T_OWN):
+            spread(chain_land[g, 2, n], near, 2 * W + OWN + 4 * n, 0)
+        rows_loop(0, T_EDGE, prepare)
+        rows_loop(0, 2 * W, middle)
+        rows_loop(3 * W, WINDOW, middle)
 
         def end(o):
             w = W + o
             own, mid = near[W + w, 0:4], near_q[W + w, 0:4]
-            right = state[w] + HALF * react(mid, win_rates[pl.ds(w, 1)])
-            parts = jnp.concatenate([0.5 * (own - mid), right, 0.5 * gather(near_q, place_w, w)[:4]], axis=1)
-            near[W + w, 0:4] = partial[w] + dot(parts, comp_w[w])
-
-        rows_loop(0, OWN, end)
-        for n in range(T_OWN):
-            end_b[g, n] = tile([near[2 * W + 4 * n + r, 0:4] for r in range(4)])
-        for copy, there in chain_copies(it, j):
-            pl.when(there)(copy.start)
-        for copy, there in value_copies(it, j):
+            right = state[w] + STEP * react(mid, win_rates[pl.ds(w, 1)])
+            parts = jnp.concatenate([own - mid, right, gather(near_q, place_w, w)[:4]], axis=1)
+            near[W + w, 0:4] = partial[w] + 0.5 * dot(parts, comp_w[w])
+
+        for half in range(2):
+            rows_loop(half * W, (half + 1) * W, end)
+            for n in range(half * T_EDGE, (half + 1) * T_EDGE):
+                end_b[g, n] = tile([near[2 * W + 4 * n + r, 0:4] for r in range(4)])
+            for copy, there in chain_copies(g, half):
+                pl.when(there)(copy.start)
+        pl.when((g == STRETCH - 1) & own_next)(lambda: value_here(g).start())
+        for copy, there in value_copies(g):
             if there is True:
                 copy.start()
             else:
@@ -742,9 +775,9 @@
         composes = jnp.where((plane == 0) & (line == 0), 1, 0)
         pl.when(on_chain & (it == composes))(window_weights)
 
-        @pl.when(on_chain & ((group < 2) == (it == 0)))
-        def _():
-            lax.fori_loop(0, ITERS * GROUP, chain_step, 0)
+        @pl.when(on_chain & (it == stretch))
+        def _():
+            lax.fori_loop(0, STRETCH, chain_step, 0)
 
         return carry
 
@@ -753,22 +786,22 @@
     weights_sent()
     for when in range(3):
         pieces(when, lambda copy: copy.wait_send())
-    for copy, there in start_copies():
-        pl.when(there)(copy.wait_send)
+    for it in range(ITERS):
+        for copy, there in start_copies(it):
+            pl.when(there)(copy.wait_send)
     terms_sent(1)
 
     @pl.when(on_chain)
     def _():
         def sent(g, carry):
-            it, j = g // GROUP, g % GROUP
-            for copy, there in chain_copies(it, j) + value_copies(it, j):
+            for copy, there in chain_copies(g, 0) + chain_copies(g, 1) + value_copies(g):
                 if there is True:
                     copy.wait_send()
                 else:
                     pl.when(there)(copy.wait_send)
             return carry
 
-        lax.fori_loop(0, ITERS * GROUP, sent, 0)
+        lax.fori_loop(0, STRETCH, sent, 0)
 
     pl.when(tm > 0)(lambda: values_wait(1, 0, False))
     values_wait(1, 1, False)
@@ -794,7 +827,7 @@
     hbm = pl.BlockSpec(memory_space=pltpu.HBM)
     dma = pltpu.SemaphoreType.DMA
     edge = W // 4
-    slots = ITERS * GROUP
+    slots = STRETCH
 
     def tiles(*lead):
         return pltpu.VMEM((*lead, 16, BS), bf16)
@@ -815,14 +848,14 @@
         pltpu.VMEM((SPECIES, 8, BS), f32), pltpu.VMEM((rows, 8, BS), f32),
         *[pltpu.VMEM((rows, SPECIES, BS), f32)] * 11, pltpu.VMEM((rows, 8, BS), f32),
         tiles(3, 2, 2 * edge), tiles(3, 2, 2 * edge),
-        tiles(ITERS, rows // 2), tiles(slots, T_WINDOW), tiles(slots, T_OWN),
+        tiles(ITERS, rows // 4, 2), tiles(slots, T_WINDOW, 2),
         tiles(rows // 4), tiles(slots, 3, T_OWN), tiles(slots, T_OWN),
         tiles(ITERS, 2, rows // 4), tiles(2, 2, edge),
         pltpu.VMEM((4, K, rows), jnp.int32), pltpu.SMEM((4, K, rows), jnp.int32),
         pltpu.SMEM((rows, K), jnp.int32), pltpu.SMEM((WINDOW, K), jnp.int32),
         dma((8,)), dma((3, 2)), dma((3, 2)), dma((4, 4)), dma((4, 4)), dma((4,)), dma((4,)),
         dma((3 * len(PIECES), 3)), dma((len(PIECES), 3)),
-        dma((ITERS, 6)), dma((slots, 3)), dma((6,)), dma((slots, 3)), dma((slots, 3)),
+        dma((ITERS, 6)), dma((slots, 3)), dma((ITERS, 6, 2)), dma((slots, 3, 2)), dma((slots, 3, 2)),
         dma((slots, 2, 2)), dma((ITERS, 2, 4)),
     ]
     return pl.pallas_call(

time: 97.2 us -> 94.6 us (0.973)
  Pallas kernels: 95.5 us -> 92.8 us
    pallas_call x1, Pallas kernels: 95.5 us -> 92.8 us  [shards(): pl.pallas_call(functools.partial(kernel, n_tm, n_sp, rows), out_shape=jax...]
where the time goes in v5:
time: 94.6 us; the launch traced here: 94.5 us
  Pallas kernels  92.8 us (98%)
  local copies, waits for them, and re-layouts  1.62 us (2%)
    pallas_call x1, Pallas kernels, shards(): pl.pallas_call(functools.partial(kernel, n_tm, n_sp, rows), out_shape=jax...  92.8 us

profile of v5, /device:TPU:120, one launch (start us, length us, event | category | flops | bytes accessed | tf_op | source)
XLA Modules:
  0.0 94.5 jit_solution(13537106172035581004)
XLA Ops:
  0.0 92.8 %shard_map.91 = f32[1,3,4,4096]{3,2,1,0:T(4,128)} custom-call(f32[4,4096]{1,0:T(4,128)} %start_h.1, f32[1,4,4096]{2,1,0:T(4,128)} %guess_h.1, s32[4,32]{1,0:T(4,128)} %bitcast.3, f32[32,128]{1,0:T(8,128)} %bitcast.2, f32[4,4]{1,0:T(4,128)} %mixing_h.1, bf16[32,128,128]{2,1,0:T(8,128)(2,1)} %diag_h.1, bf16[32,4,128,128]{3,2,1,0:T(8,128)(2,1)} %off_h.1, ...), custom_call_target="tpu_custom_call" | custom-call | tf_op jit(solution)/shard_map/pallas_call | solution.py:861
  92.8 1.6 %copy.11 = f32[1,3,4,4096]{3,2,1,0:T(4,128)} copy(f32[1,3,4,4096]{3,2,1,0:T(4,128)} %shard_map.91) | data formatting | bytes 393216

commit v6 on v5

--- a/solution.py
+++ b/solution.py
@@ -406,6 +406,7 @@
         def _():
             halo_send(NODES, [lambda b: nodes[b, 0:4], lambda b: nodes[b, 4:8]])
             first_things()
+            pl.when(tm == 0)(start_out)
             for load in large:
                 load.wait()
             lax.fori_loop(0, rows // 4, transposed, 0)
@@ -463,7 +464,6 @@
 
         outer(node_terms, solve(first_v))
         halo_send(FIRST, [lambda b: first_v[b]])
-        pl.when((it == 0) & (tm == 0))(start_out)
         inner(node_terms, solve(first_v))
 
         def put_first(b):
@@ -488,12 +488,6 @@
 
         outer(first_terms, solve(fresh))
         halo_send(SECOND, [lambda b: fresh[b]])
-
-        @pl.when((it == 0) & (tm == 0))
-        def _():
-            for copy, there in start_copies(1):
-                pl.when(there)(copy.start)
-
         inner(first_terms, solve(fresh))
 
         def put_second(b):
@@ -768,6 +762,12 @@
         @pl.when(it == 0)
         def _():
             terms_sent(0)
+
+            @pl.when(tm == 0)
+            def _():
+                for copy, there in start_copies(1):
+                    pl.when(there)(copy.start)
+
             pieces(1, lambda copy: copy.start())
             pieces(2, lambda copy: copy.start())
             pl.when(plane != first_plane)(weights_out)

time: 94.6 us -> 94.6 us (level)
  no operation moved by 1% of the time
where the time goes in v6:
time: 94.6 us; the launch traced here: 94.4 us
  Pallas kernels  92.8 us (98%)
  local copies, waits for them, and re-layouts  1.62 us (2%)
    pallas_call x1, Pallas kernels, shards(): pl.pallas_call(functools.partial(kernel, n_tm, n_sp, rows), out_shape=jax...  92.8 us

profile of v6, /device:TPU:120, one launch (start us, length us, event | category | flops | bytes accessed | tf_op | source)
XLA Modules:
  0.0 94.4 jit_solution(1063997168941475744)
XLA Ops:
  0.0 92.8 %shard_map.91 = f32[1,3,4,4096]{3,2,1,0:T(4,128)} custom-call(f32[4,4096]{1,0:T(4,128)} %start_h.1, f32[1,4,4096]{2,1,0:T(4,128)} %guess_h.1, s32[4,32]{1,0:T(4,128)} %bitcast.3, f32[32,128]{1,0:T(8,128)} %bitcast.2, f32[4,4]{1,0:T(4,128)} %mixing_h.1, bf16[32,128,128]{2,1,0:T(8,128)(2,1)} %diag_h.1, bf16[32,4,128,128]{3,2,1,0:T(8,128)(2,1)} %off_h.1, ...), custom_call_target="tpu_custom_call" | custom-call | tf_op jit(solution)/shard_map/pallas_call | solution.py:861
  92.8 1.6 %copy.11 = f32[1,3,4,4096]{3,2,1,0:T(4,128)} copy(f32[1,3,4,4096]{3,2,1,0:T(4,128)} %shard_map.91) | data formatting | bytes 393216

commit v7 on v6

--- a/solution.py
+++ b/solution.py
@@ -713,6 +713,12 @@
 
         rows_loop(0, T_OWN, with_rest)
 
+        def far_part(w):
+            partial[w] = 0.5 * dot(gather(near, place_w, w), comp_w[w, 2 * BS :])[:4]
+
+        def middle_sum(w):
+            near_q[W + w, 0:4] = solved[w] + 2.0 * partial[w]
+
         def middle(w):
             spread_s = dot(gather(near, place_w, w), comp_w[w, 2 * BS :])[:4]
             near_q[W + w, 0:4] = solved[w] + spread_s
@@ -722,8 +728,8 @@
         arrive(chain_land.at[g, 2, first], chain_recv.at[g, 2, 0], chunk_right)
         for n in range(T_EDGE):
             spread(chain_land[g, 2, n], near, 2 * W + OWN + 4 * n, 0)
+        rows_loop(2 * W, 2 * W + W, middle)
         rows_loop(T_WINDOW - T_EDGE, T_WINDOW, prepare)
-        rows_loop(2 * W, 2 * W + W, middle)
         arrive(chain_land.at[g, 0, first], chain_recv.at[g, 0, 0], chunk_left)
         arrive(chain_land.at[g, 0, last], chain_recv.at[g, 0, 1], chunk_left)
         arrive(chain_land.at[g, 2, last], chain_recv.at[g, 2, 1], chunk_right)
@@ -731,18 +737,24 @@
             spread(chain_land[g, 0, n], near, 4 * n, 0)
         for n in range(T_EDGE, T_OWN):
             spread(chain_land[g, 2, n], near, 2 * W + OWN + 4 * n, 0)
+        rows_loop(0, W, far_part)
         rows_loop(0, T_EDGE, prepare)
-        rows_loop(0, 2 * W, middle)
+        rows_loop(W, 2 * W, middle)
+        rows_loop(0, W, middle_sum)
         rows_loop(3 * W, WINDOW, middle)
+
+        def end_far(o):
+            fresh[o] = dot(gather(near_q, place_w, W + o), comp_w[W + o, 2 * BS :])[:4]
 
         def end(o):
             w = W + o
             own, mid = near[W + w, 0:4], near_q[W + w, 0:4]
             right = state[w] + STEP * react(mid, win_rates[pl.ds(w, 1)])
-            parts = jnp.concatenate([own - mid, right, gather(near_q, place_w, w)[:4]], axis=1)
-            near[W + w, 0:4] = partial[w] + 0.5 * dot(parts, comp_w[w])
+            parts = jnp.concatenate([own - mid, right], axis=1)
+            near[W + w, 0:4] = partial[w] + 0.5 * (fresh[o] + dot(parts, comp_w[w, : 2 * BS]))
 
         for half in range(2):
+            rows_loop(half * W, (half + 1) * W, end_far)
             rows_loop(half * W, (half + 1) * W, end)
             for n in range(half * T_EDGE, (half + 1) * T_EDGE):
                 end_b[g, n] = tile([near[2 * W + 4 * n + r, 0:4] for r in range(4)])
@@ -804,17 +816,24 @@
         lax.fori_loop(0, STRETCH, sent, 0)
 
     pl.when(tm > 0)(lambda: values_wait(1, 0, False))
-    values_wait(1, 1, False)
-
-    def write(j):
-        ends = value_land[1, 1, j].astype(jnp.float32)
+
+    def write_start(j):
         starts = value_land[1, 0, j].astype(jnp.float32)
         for g in range(4):
             b = 4 * j + g
             own = jnp.where(tm == 0, start[:, cells(b)], starts[4 * g : 4 * g + 4])
+            out[0, 0, :, cells(b)] = own
+            mid_b[b] += 0.5 * own
+
+    rows_loop(0, rows // 4, write_start)
+    values_wait(1, 1, False)
+
+    def write(j):
+        ends = value_land[1, 1, j].astype(jnp.float32)
+        for g in range(4):
+            b = 4 * j + g
             last = ends[4 * g : 4 * g + 4]
-            out[0, 0, :, cells(b)] = own
-            out[0, 1, :, cells(b)] = mid_b[b] + 0.5 * (own + last)
+            out[0, 1, :, cells(b)] = mid_b[b] + 0.5 * last
             out[0, 2, :, cells(b)] = last
 
     rows_loop(0, rows // 4, write)

time: 94.6 us -> 94.5 us (level)
  no operation moved by 1% of the time
where the time goes in v7:
time: 94.5 us; the launch traced here: 94.3 us
  Pallas kernels  92.7 us (98%)
  local copies, waits for them, and re-layouts  1.62 us (2%)
    pallas_call x1, Pallas kernels, shards(): pl.pallas_call(functools.partial(kernel, n_tm, n_sp, rows), out_shape=jax...  92.7 us

profile of v7, /device:TPU:120, one launch (start us, length us, event | category | flops | bytes accessed | tf_op | source)
XLA Modules:
  0.0 94.3 jit_solution(6288245248583609360)
XLA Ops:
  0.0 92.7 %shard_map.91 = f32[1,3,4,4096]{3,2,1,0:T(4,128)} custom-call(f32[4,4096]{1,0:T(4,128)} %start_h.1, f32[1,4,4096]{2,1,0:T(4,128)} %guess_h.1, s32[4,32]{1,0:T(4,128)} %bitcast.3, f32[32,128]{1,0:T(8,128)} %bitcast.2, f32[4,4]{1,0:T(4,128)} %mixing_h.1, bf16[32,128,128]{2,1,0:T(8,128)(2,1)} %diag_h.1, bf16[32,4,128,128]{3,2,1,0:T(8,128)(2,1)} %off_h.1, ...), custom_call_target="tpu_custom_call" | custom-call | tf_op jit(solution)/shard_map/pallas_call | solution.py:880
  92.7 1.6 %copy.11 = f32[1,3,4,4096]{3,2,1,0:T(4,128)} copy(f32[1,3,4,4096]{3,2,1,0:T(4,128)} %shard_map.91) | data formatting | bytes 393216
